TPU v7x, 32 devices: a whole 2x2x4 slice. The times are simulated.
32 devices in a mesh: dp: 4 (over y, core), mp: 8 (over z, x).
Axes of the slice: x: 2, y: 2, z: 4, core: 2. Of those that a mesh axis runs over, the one named last changes fastest.
Arguments:
- tokens: bfloat16 [1024, 1024], P('dp'), may hold values from -6 to 6
- lengths: int32 [4], P('dp'), may hold values from 64 to 256
- cotangent: bfloat16 [1024, 1024], P('dp'), may hold values from -6 to 6
- triple_weight: bfloat16 [2, 1024, 3, 1024], P(None, None, None, 'mp'), may hold values from -0.1875 to 0.1875
- output_weight: bfloat16 [2, 1024, 1024], P(None, None, 'mp'), may hold values from -0.1875 to 0.1875
- upward_weight: bfloat16 [2, 1024, 4096], P(None, None, 'mp'), may hold values from -0.1875 to 0.1875
- downward_weight: bfloat16 [2, 1024, 4096], P(None, None, 'mp'), may hold values from -0.09375 to 0.09375
Outputs:
- final_stream: bfloat16 [1024, 1024], P('dp')
- triple_grad: float32 [2, 1024, 3, 1024], P(None, 'dp', None, 'mp')
- output_grad: float32 [2, 1024, 1024], P(None, 'dp', 'mp')
- upward_grad: float32 [2, 1024, 4096], P(None, 'dp', 'mp')
- downward_grad: float32 [2, 1024, 4096], P(None, 'dp', 'mp')
Inputs may be any that keep to these rules, and one draw needn't show every extreme that they name: lengths[s] counts the live candidates of slate s; its other positions are padding.
All inputs are finite; a program needn't handle non-finite values.
Results may differ from a plain program's by a relative error of at most 0.04.
Values may be sent and summed in bfloat16 or wider, within the bound.
A program may use at most 64 MiB of HBM per device.

v0:
```python
import jax
import jax.numpy as jnp
from jax import lax
from jax.sharding import PartitionSpec as P

HD = 64
SLATE = 256
LAYERS = 2


epsilon = 1e-06


def normalize(stream):
    widened = stream.astype(jnp.float32)
    rscale = lax.rsqrt(jnp.mean(widened * widened, axis=-1, keepdims=True) + epsilon)
    scaled = widened * rscale
    return (scaled.astype(jnp.bfloat16), scaled, rscale)


def norm_backward(scaled, rscale, upward):
    inner = jnp.mean(upward * scaled, axis=-1, keepdims=True)
    return rscale * (upward - scaled * inner)


def smooth_gate(preact):
    return jax.nn.gelu(preact, approximate=True)


def attend(queries, key_rows, values, lengths):
    live_keys = (jnp.arange(SLATE)[None, :] < lengths[:, None]).astype(jnp.float32)
    scores = jnp.einsum(
        "bqhe,bkhe->bhqk", queries, key_rows, preferred_element_type=jnp.float32
    ) * HD ** (-0.5)
    weights = jnp.exp(scores) * live_keys[:, None, None, :]
    probs = weights / jnp.sum(weights, axis=-1, keepdims=True)
    probs_low = probs.astype(jnp.bfloat16)
    context = jnp.einsum(
        "bhqk,bkhe->bqhe", probs_low, values, preferred_element_type=jnp.float32
    ).astype(jnp.bfloat16)
    return (probs, probs_low, context)


def attend_backward(probs, probs_low, queries, key_rows, values, grad_context):
    grad_prob = jnp.einsum(
        "bqhe,bkhe->bhqk", grad_context, values, preferred_element_type=jnp.float32
    )
    grad_value = jnp.einsum(
        "bhqk,bqhe->bkhe", probs_low, grad_context, preferred_element_type=jnp.float32
    ).astype(jnp.bfloat16)
    inner = jnp.sum(grad_prob * probs, axis=-1, keepdims=True)
    grad_score = (probs * (grad_prob - inner) * HD ** (-0.5)).astype(jnp.bfloat16)
    grad_query = jnp.einsum(
        "bhqk,bkhe->bqhe", grad_score, key_rows, preferred_element_type=jnp.float32
    ).astype(jnp.bfloat16)
    grad_key = jnp.einsum(
        "bhqk,bqhe->bkhe", grad_score, queries, preferred_element_type=jnp.float32
    ).astype(jnp.bfloat16)
    return (grad_query, grad_key, grad_value)


def contract_rows(left, right):
    return lax.dot_general(
        left, right, (((0,), (0,)), ((), ())), preferred_element_type=jnp.float32
    )


def contract_cols(left, right):
    return lax.dot_general(
        left, right, (((1,), (1,)), ((), ())), preferred_element_type=jnp.float32
    )


def body(tokens, lengths, cotangent, triple_weight, output_weight, upward_weight, downward_weight):
    row_count = tokens.shape[0]
    slates = row_count // SLATE
    model_width = tokens.shape[1]
    heads_here = triple_weight.shape[-1] // HD
    stream = tokens
    normed, scaled, rscale = normalize(tokens)
    final_stream = tokens
    saved = []
    for layer_index in range(LAYERS):
        flat_triple = triple_weight[layer_index].reshape(model_width, -1)
        qkv = jnp.dot(normed, flat_triple, preferred_element_type=jnp.float32).astype(jnp.bfloat16)
        shaped = qkv.reshape(slates, SLATE, 3, heads_here, HD)
        queries = shaped[:, :, 0]
        key_rows = shaped[:, :, 1]
        values = shaped[:, :, 2]
        probs, probs_low, context = attend(queries, key_rows, values, lengths)
        context_flat = context.reshape(row_count, -1)
        partial_att = contract_cols(context_flat, output_weight[layer_index])
        attn_sum = lax.psum(partial_att.astype(jnp.bfloat16), "mp").astype(jnp.float32)
        mid_stream = (stream.astype(jnp.float32) + attn_sum).astype(jnp.bfloat16)
        normed_mid, scaled_mid, rscale_mid = normalize(mid_stream)
        preact = jnp.dot(normed_mid, upward_weight[layer_index], preferred_element_type=jnp.float32)
        activated = smooth_gate(preact).astype(jnp.bfloat16)
        partial_ffn = contract_cols(activated, downward_weight[layer_index])
        saved.append(
            (
                normed,
                scaled,
                rscale,
                queries,
                key_rows,
                values,
                probs,
                probs_low,
                context_flat,
                scaled_mid,
                rscale_mid,
                normed_mid,
                preact,
                activated,
            )
        )
        ffn_sum = lax.psum(partial_ffn.astype(jnp.bfloat16), "mp").astype(jnp.float32)
        stream = (mid_stream.astype(jnp.float32) + ffn_sum).astype(jnp.bfloat16)
        normed, scaled, rscale = normalize(stream)
        final_stream = stream
    gradients = []
    upstream = cotangent
    for layer_index in reversed(range(LAYERS)):
        (
            normed,
            scaled,
            rscale,
            queries,
            key_rows,
            values,
            probs,
            probs_low,
            context_flat,
            scaled_mid,
            rscale_mid,
            normed_mid,
            preact,
            activated,
        ) = saved[layer_index]
        downward_grad = contract_rows(upstream, activated)
        grad_act = jnp.dot(
            upstream, downward_weight[layer_index], preferred_element_type=jnp.float32
        ).astype(jnp.bfloat16)
        _, gate_back = jax.vjp(smooth_gate, preact)
        grad_preact = gate_back(grad_act.astype(jnp.float32))[0].astype(jnp.bfloat16)
        upward_grad = contract_rows(normed_mid, grad_preact)
        grad_normed = lax.psum(
            contract_cols(grad_preact, upward_weight[layer_index]).astype(jnp.bfloat16), "mp"
        ).astype(jnp.float32)
        grad_mid = (
            upstream.astype(jnp.float32) + norm_backward(scaled_mid, rscale_mid, grad_normed)
        ).astype(jnp.bfloat16)
        output_grad = contract_rows(grad_mid, context_flat)
        grad_context = jnp.dot(
            grad_mid, output_weight[layer_index], preferred_element_type=jnp.float32
        ).astype(jnp.bfloat16)
        grad_query, grad_key, grad_value = attend_backward(
            probs,
            probs_low,
            queries,
            key_rows,
            values,
            grad_context.reshape(slates, SLATE, heads_here, HD),
        )
        grad_qkv = jnp.stack([grad_query, grad_key, grad_value], axis=2).reshape(row_count, -1)
        triple_grad = contract_rows(normed, grad_qkv).reshape(model_width, 3, -1)
        pieces = (triple_grad, output_grad, upward_grad, downward_grad)
        gradients.insert(0, pieces)
        if layer_index > 0:
            flat_triple = triple_weight[layer_index].reshape(model_width, -1)
            grad_input = lax.psum(
                contract_cols(grad_qkv, flat_triple).astype(jnp.bfloat16), "mp"
            ).astype(jnp.float32)
            upstream = (
                grad_mid.astype(jnp.float32) + norm_backward(scaled, rscale, grad_input)
            ).astype(jnp.bfloat16)
    stacked = tuple(
        (
            jnp.stack([gradients[layer_pos][slot_index] for layer_pos in range(LAYERS)])
            for slot_index in range(4)
        )
    )
    merged = (
        lax.psum_scatter(
            stacked[0].astype(jnp.bfloat16), "dp", scatter_dimension=1, tiled=True
        ).astype(jnp.float32),
        lax.psum_scatter(
            stacked[1].astype(jnp.bfloat16), "dp", scatter_dimension=1, tiled=True
        ).astype(jnp.float32),
        lax.psum_scatter(
            stacked[2].astype(jnp.bfloat16), "dp", scatter_dimension=1, tiled=True
        ).astype(jnp.float32),
        lax.psum_scatter(
            stacked[3].astype(jnp.bfloat16), "dp", scatter_dimension=1, tiled=True
        ).astype(jnp.float32),
    )
    return (final_stream, merged[0], merged[1], merged[2], merged[3])


def solution(mesh):
    placed = (
        P("dp", None),
        P("dp"),
        P("dp", None),
        P(None, None, None, "mp"),
        P(None, None, "mp"),
        P(None, None, "mp"),
        P(None, None, "mp"),
    )
    return jax.shard_map(
        body,
        mesh=mesh,
        in_specs=placed,
        out_specs=(
            P("dp", None),
            P(None, "dp", None, "mp"),
            P(None, "dp", "mp"),
            P(None, "dp", "mp"),
            P(None, "dp", "mp"),
        ),
        check_vma=False,
    )
```

profile of v0, /device:TPU:0, one launch (start us, length us, event | category | flops | bytes accessed | tf_op | source)
XLA Modules:
  0.0 626.1 jit_solution(13629008110707455821)
XLA Ops:
  7.9 1.5 fusion.151
  12.7 75.2 %all-reduce.8.cloned.1.call-done = bf16[256,1024]{1,0:T(8,128)(2,1)} async-done(((bf16[256,1024]{1,0:T(8,128)(2,1)}), bf16[256,1024]{1,0:T(8,128)(2,1)}) %all-reduce.8.cloned.1.call-update) | async-done | bytes 524304 | tf_op jit(solution)/shard_map/psum | solution.py:93
  87.8 1.5 fusion.54
  89.3 1.7 fusion.68
  92.7 71.5 %all-reduce.10.cloned.1.call-done = bf16[256,1024]{1,0:T(8,128)(2,1)} async-done(((bf16[256,1024]{1,0:T(8,128)(2,1)}), bf16[256,1024]{1,0:T(8,128)(2,1)}) %all-reduce.10.cloned.1.call-update) | async-done | bytes 524304 | tf_op jit(solution)/shard_map/psum | solution.py:117
  170.3 71.7 %all-reduce.12.cloned.1.call-done = bf16[256,1024]{1,0:T(8,128)(2,1)} async-done(((bf16[256,1024]{1,0:T(8,128)(2,1)}), bf16[256,1024]{1,0:T(8,128)(2,1)}) %all-reduce.12.cloned.1.call-update) | async-done | bytes 524304 | tf_op jit(solution)/shard_map/psum | solution.py:93
  242.1 1.5 fusion.58
  243.5 1.7 fusion.63
  249.0 71.8 %all-reduce.14.cloned.1.call-done = bf16[256,1024]{1,0:T(8,128)(2,1)} async-done(((bf16[256,1024]{1,0:T(8,128)(2,1)}), bf16[256,1024]{1,0:T(8,128)(2,1)}) %all-reduce.14.cloned.1.call-update) | async-done | bytes 524304 | tf_op jit(solution)/shard_map/psum | solution.py:147
  322.1 1.6 fusion.41
  324.9 1.9 fusion.35
  326.8 1.9 fusion.135
  328.7 2.4 fusion.34
  331.1 2.4 fusion.33
  336.5 2.7 convolution_convert_fusion.9
  339.2 69.1 %all-reduce.16.cloned.1.call-done = bf16[256,1024]{1,0:T(8,128)(2,1)} async-done(((bf16[256,1024]{1,0:T(8,128)(2,1)}), bf16[256,1024]{1,0:T(8,128)(2,1)}) %all-reduce.16.cloned.1.call-update) | async-done | bytes 524304 | tf_op jit(solution)/shard_map/psum | solution.py:171
  408.2 1.5 fusion.49
  416.0 1.5 fusion.16
  417.5 75.3 %all-reduce.18.cloned.1.call-done = (bf16[256,1024]{1,0:T(8,128)(2,1)}, bf16[256,1024]{1,0:T(8,128)(2,1)}) async-done(((bf16[256,1024]{1,0:T(8,128)(2,1)}, bf16[256,1024]{1,0:T(8,128)(2,1)}), (bf16[256,1024]{1,0:T(8,128)(2,1)}, bf16[256,1024]{1,0:T(8,128)(2,1)})) %all-reduce.18.cloned.1.call-update) | async-done | bytes 1048592 | tf_op jit(solution)/shard_map/psum | solution.py:117
  492.7 1.4 fusion.50
  494.1 1.6 fusion.47
  500.7 1.7 fusion.36
  506.9 1.5 pad_maximum_fusion
  510.9 1.5 pad_maximum_fusion.1
  514.4 3.8 reduce-scatter.7.cloned.1.call-done
  518.1 1.6 convert_element_type.324
  519.8 29.3 %reduce-scatter.5.cloned.1.call-done = bf16[2,256,3,128]{3,1,2,0:T(8,128)(2,1)} async-done(((bf16[2,1024,3,128]{3,1,2,0:T(8,128)(2,1)}), bf16[2,256,3,128]{3,1,2,0:T(8,128)(2,1)}) %reduce-scatter.5.cloned.1.call-update) | async-done | bytes 393232 | tf_op jit(solution)/shard_map/reduce_scatter | solution.py:184
  549.1 1.9 convert_element_type.323
  551.0 32.1 %reduce-scatter.9.cloned.1.call-done = bf16[2,256,512]{2,1,0:T(8,128)(2,1)} async-done(((bf16[2,1024,512]{2,1,0:T(8,128)(2,1)}), bf16[2,256,512]{2,1,0:T(8,128)(2,1)}) %reduce-scatter.9.cloned.1.call-update) | async-done | bytes 524304 | tf_op jit(solution)/shard_map/reduce_scatter | solution.py:190
  583.1 2.1 convert_element_type.325
  585.2 31.9 %reduce-scatter.11.cloned.1.call-done = bf16[2,256,512]{2,1,0:T(8,128)(2,1)} async-done(((bf16[2,1024,512]{2,1,0:T(8,128)(2,1)}), bf16[2,256,512]{2,1,0:T(8,128)(2,1)}) %reduce-scatter.11.cloned.1.call-update) | async-done | bytes 524304 | tf_op jit(solution)/shard_map/reduce_scatter | solution.py:193
  617.1 2.1 convert_element_type.326
  (121 shorter events, 40.1 us)
Async XLA Ops:
  7.2 80.7 %all-reduce.8.cloned.1.call-start = ((), (), s32[]{:S(2)}) async-start(), calls=%async_computation.4 | async-start | bytes 1048576 | tf_op jit(solution)/shard_map/psum | solution.py:93
  7.9 1.8 copy-start
  10.4 1.0 copy-start.6
  10.6 2.0 copy-start.11
  10.9 1.7 copy-start.3
  12.6 151.5 %all-reduce.10.cloned.1.call-start = ((), (), s32[]{:S(2)}) async-start(), calls=%async_computation.5 | async-start | bytes 1048576 | tf_op jit(solution)/shard_map/psum | solution.py:117
  87.8 3.2 copy-start.19
  91.0 1.4 copy-start.24
  92.3 149.7 %all-reduce.12.cloned.1.call-start = ((), (), s32[]{:S(2)}) async-start(), calls=%async_computation.6 | async-start | bytes 1048576 | tf_op jit(solution)/shard_map/psum | solution.py:93
  168.0 2.3 copy-start.5
  170.2 75.8 %copy-start.7 = (bf16[256,1024]{1,0:T(8,128)(2,1)S(1)}, bf16[256,1024]{1,0:T(8,128)(2,1)}, u32[]{:S(2)}) copy-start(bf16[256,1024]{1,0:T(8,128)(2,1)} %param.9) | copy-start | bytes 1572868
  170.3 150.5 %all-reduce.14.cloned.1.call-start = ((), (), s32[]{:S(2)}) async-start(), calls=%async_computation.7 | async-start | bytes 1048576 | tf_op jit(solution)/shard_map/psum | solution.py:147
  242.0 4.0 copy-start.20
  246.0 1.6 copy-start.22
  248.9 159.3 %all-reduce.16.cloned.1.call-start = ((), (), s32[]{:S(2)}) async-start(), calls=%async_computation.8 | async-start | bytes 1048576 | tf_op jit(solution)/shard_map/psum | solution.py:171
  336.4 156.3 %all-reduce.18.cloned.1.call-start = ((), (), s32[]{:S(2)}) async-start(), calls=%async_computation.13 | async-start | bytes 2097152 | tf_op jit(solution)/shard_map/psum | solution.py:117
  339.2 72.8 %copy-start.25 = (f32[256,512]{1,0:T(8,128)S(1)}, f32[256,512]{1,0:T(8,128)}, u32[]{:S(2)}) copy-start(f32[256,512]{1,0:T(8,128)} %copy-done.24) | copy-start | bytes 1572868
  408.2 3.7 copy-start.21
  412.0 1.6 copy-start.23
  413.6 2.4 copy-start.17
  414.9 103.3 %reduce-scatter.7.cloned.1.call-start = ((), (), s32[]{:S(2)}) async-start(), calls=%async_computation.10 | async-start | bytes 655360 | tf_op jit(solution)/shard_map/reduce_scatter | solution.py:187
  492.7 3.3 copy-start.10
  495.7 3.9 copy-start.4
  496.9 52.1 %reduce-scatter.5.cloned.1.call-start = ((), (), s32[]{:S(2)}) async-start(), calls=%async_computation.9 | async-start | bytes 1966080 | tf_op jit(solution)/shard_map/reduce_scatter | solution.py:184
  504.1 1.4 copy-start.16
  505.4 77.7 %reduce-scatter.9.cloned.1.call-start = ((), (), s32[]{:S(2)}) async-start(), calls=%async_computation.11 | async-start | bytes 2621440 | tf_op jit(solution)/shard_map/reduce_scatter | solution.py:190
  508.4 1.0 copy-start.8
  508.4 1.2 copy-start.14
  508.4 1.8 copy-start.2
  508.4 1.8 copy-start.26
  508.5 108.6 %reduce-scatter.11.cloned.1.call-start = ((), (), s32[]{:S(2)}) async-start(), calls=%async_computation.12 | async-start | bytes 2621440 | tf_op jit(solution)/shard_map/reduce_scatter | solution.py:193
  512.3 1.0 copy-start.12
  (5 other events, 3.9 us)
Sparse Core Ops, SparseCore 0:
  12.7 75.0 all-reduce.7
  92.4 71.6 all-reduce.9
  170.4 71.6 all-reduce.11
  249.0 71.6 all-reduce.13
  336.6 71.6 all-reduce.15
  415.0 77.6 all-reduce.17
  497.1 21.0 reduce-scatter.6
  520.8 28.1 reduce-scatter.4
  551.6 31.4 reduce-scatter.8
  585.6 31.4 reduce-scatter.10
where the time goes:
time: 628 us; the launch traced here: 626 us
  waiting for transfers between devices  532 us (85%)
  matrix products  39.6 us (6%)
  other arithmetic  29 us (5%)
  between operations  15.2 us (2%)
  local copies, waits for them, and re-layouts  10 us (2%)
    psum x2, waiting for transfers between devices, body(): lax.psum(partial_att.astype(jnp.bfloat16), 'mp').astype(jnp.float32)  147 us
    psum x2, waiting for transfers between devices, body(): lax.psum(partial_ffn.astype(jnp.bfloat16), 'mp').astype(jnp.float32)  147 us
    psum x1, waiting for transfers between devices, body(): lax.psum(contract_cols(grad_preact, upward_weight[layer_index]).astype(jn...  71.8 us
    psum x1, waiting for transfers between devices, body(): lax.psum(contract_cols(grad_qkv, flat_triple).astype(jnp.bfloat16), 'mp')  69.1 us
    reduce_scatter x1, waiting for transfers between devices, body(): lax.psum_scatter(stacked[2].astype(jnp.bfloat16), 'dp', scatter_dimension...  32.1 us
    reduce_scatter x1, waiting for transfers between devices, body(): lax.psum_scatter(stacked[3].astype(jnp.bfloat16), 'dp', scatter_dimension...  31.9 us
    reduce_scatter x1, waiting for transfers between devices, body(): lax.psum_scatter(stacked[0].astype(jnp.bfloat16), 'dp', scatter_dimension...  29.3 us
  transfers between devices with their start and end apart: 10, of which 10 were waited for; matrix products, arithmetic and copies ran while one was open for 4% of the time, Pallas kernels for 0%

commit v1 on v0

--- a/solution.py
+++ b/solution.py
@@ -1,11 +1,16 @@
+import functools
+
 import jax
 import jax.numpy as jnp
 from jax import lax
+from jax.experimental import pallas as pl
+from jax.experimental.pallas import tpu as pltpu
 from jax.sharding import PartitionSpec as P
 
 HD = 64
 SLATE = 256
 LAYERS = 2
+MESH = pl.DeviceIdType.MESH
 
 
 epsilon = 1e-06
@@ -71,16 +76,141 @@
     )
 
 
-def body(tokens, lengths, cotangent, triple_weight, output_weight, upward_weight, downward_weight):
+def remote(src, dst, send_sem, recv_sem, axis, device):
+    return pltpu.make_async_remote_copy(
+        src_ref=src,
+        dst_ref=dst,
+        send_sem=send_sem,
+        recv_sem=recv_sem,
+        device_id={axis: device},
+        device_id_type=MESH,
+    )
+
+
+def place(axis, n):
+    me = lax.axis_index(axis)
+    parity = lax.rem(me, 2)
+    group = lax.div(me, 2)
+    partner = me + 1 - 2 * parity
+    groups = n // 2
+    return me, parity, group, partner, groups
+
+
+def greet(axis, n):
+    me, parity, group, partner, groups = place(axis, n)
+    barrier = pltpu.get_barrier_semaphore()
+    pl.semaphore_signal(barrier, inc=1, device_id={axis: partner}, device_id_type=MESH)
+    for j in range(1, groups):
+        peer = lax.rem(group + j, groups) * 2 + parity
+        pl.semaphore_signal(barrier, inc=1, device_id={axis: peer}, device_id_type=MESH)
+    return groups
+
+
+def sum_scatter(axis, n, part, first, held, second, sems):
+    me, parity, group, partner, groups = place(axis, n)
+    to_pair, to_peer = [None] * groups, [None] * groups
+    order = list(range(1, groups)) + [0]
+    for j in order:
+        there = lax.rem(group + j, groups) * 2
+        to_pair[j] = remote(
+            part.at[there + 1 - parity], first.at[j], sems.at[0, j], sems.at[1, j], axis, partner
+        )
+        to_pair[j].start()
+    for j in order[:-1]:
+        peer = lax.rem(group + j, groups) * 2 + parity
+        to_pair[j].wait_recv()
+        held[j] = (part[peer].astype(jnp.float32) + first[j].astype(jnp.float32)).astype(held.dtype)
+        to_peer[j] = remote(held.at[j], second.at[j], sems.at[2, j], sems.at[3, j], axis, peer)
+        to_peer[j].start()
+    to_pair[0].wait_recv()
+    total = part[me].astype(jnp.float32) + first[0].astype(jnp.float32)
+    for j in order[:-1]:
+        to_peer[j].wait_recv()
+        total = total + second[j].astype(jnp.float32)
+    return total, to_pair + to_peer[1:]
+
+
+def spread(axis, n, whole, sems):
+    me, parity, group, partner, groups = place(axis, n)
+    sent = []
+    for j in range(1, groups):
+        peer = lax.rem(group + j, groups) * 2 + parity
+        copy = remote(whole.at[me], whole.at[me], sems.at[4, j], sems.at[5, j], axis, peer)
+        copy.start()
+        sent.append(copy)
+    across = [remote(whole.at[me], whole.at[me], sems.at[6, 0], sems.at[7, 0], axis, partner)]
+    across[0].start()
+    for j in range(1, groups):
+        sent[j - 1].wait_recv()
+        owner = lax.rem(group + groups - j, groups) * 2 + parity
+        copy = remote(whole.at[owner], whole.at[owner], sems.at[6, j], sems.at[7, j], axis, partner)
+        copy.start()
+        across.append(copy)
+    for copy in across:
+        copy.wait_recv()
+    return sent + across
+
+
+def forward_sum(n, part, stream, out, first, held, second, whole, sems):
+    me = lax.axis_index("mp")
+    pl.semaphore_wait(pltpu.get_barrier_semaphore(), greet("mp", n))
+    total, copies = sum_scatter("mp", n, part, first, held, second, sems)
+    whole[me] = (stream[me].astype(jnp.float32) + total).astype(whole.dtype)
+    copies = copies + spread("mp", n, whole, sems)
+    for copy in copies:
+        copy.wait_send()
+    out[...] = whole[...]
+
+
+def backward_sum(n, part, stream, upstream, out, first, held, second, whole, sems):
+    me = lax.axis_index("mp")
+    pl.semaphore_wait(pltpu.get_barrier_semaphore(), greet("mp", n))
+    total, copies = sum_scatter("mp", n, part, first, held, second, sems)
+    _, scaled, rscale = normalize(stream[me])
+    whole[me] = (
+        upstream[me].astype(jnp.float32) + norm_backward(scaled, rscale, total)
+    ).astype(whole.dtype)
+    copies = copies + spread("mp", n, whole, sems)
+    for copy in copies:
+        copy.wait_send()
+    out[...] = whole[...]
+
+
+def summed(kernel, collective_id, n, part, *rest):
+    rows, columns = part.shape
+    chunk = rows // n
+    cut = (n, chunk, columns)
+    half = (n // 2, chunk, columns)
+    vmem = pl.BlockSpec(memory_space=pltpu.VMEM)
+    operands = [array.reshape(cut) for array in (part,) + rest]
+    out = pl.pallas_call(
+        functools.partial(kernel, n),
+        out_shape=jax.ShapeDtypeStruct(cut, part.dtype),
+        in_specs=[vmem] * len(operands),
+        out_specs=vmem,
+        scratch_shapes=[
+            pltpu.VMEM(half, part.dtype),
+            pltpu.VMEM(half, part.dtype),
+            pltpu.VMEM(half, part.dtype),
+            pltpu.VMEM(cut, part.dtype),
+            pltpu.SemaphoreType.DMA((8, n // 2)),
+        ],
+        compiler_params=pltpu.CompilerParams(
+            collective_id=collective_id, has_side_effects=True, vmem_limit_bytes=16 << 20
+        ),
+    )(*operands)
+    return out.reshape(rows, columns)
+
+
+def body(n, tokens, lengths, cotangent, triple_weight, output_weight, upward_weight, downward_weight):
     row_count = tokens.shape[0]
     slates = row_count // SLATE
     model_width = tokens.shape[1]
     heads_here = triple_weight.shape[-1] // HD
     stream = tokens
-    normed, scaled, rscale = normalize(tokens)
-    final_stream = tokens
     saved = []
     for layer_index in range(LAYERS):
+        normed, _, _ = normalize(stream)
         flat_triple = triple_weight[layer_index].reshape(model_width, -1)
         qkv = jnp.dot(normed, flat_triple, preferred_element_type=jnp.float32).astype(jnp.bfloat16)
         shaped = qkv.reshape(slates, SLATE, 3, heads_here, HD)
@@ -90,49 +220,42 @@
         probs, probs_low, context = attend(queries, key_rows, values, lengths)
         context_flat = context.reshape(row_count, -1)
         partial_att = contract_cols(context_flat, output_weight[layer_index])
-        attn_sum = lax.psum(partial_att.astype(jnp.bfloat16), "mp").astype(jnp.float32)
-        mid_stream = (stream.astype(jnp.float32) + attn_sum).astype(jnp.bfloat16)
-        normed_mid, scaled_mid, rscale_mid = normalize(mid_stream)
+        mid_stream = summed(forward_sum, 0, n, partial_att.astype(jnp.bfloat16), stream)
+        normed_mid, _, _ = normalize(mid_stream)
         preact = jnp.dot(normed_mid, upward_weight[layer_index], preferred_element_type=jnp.float32)
         activated = smooth_gate(preact).astype(jnp.bfloat16)
         partial_ffn = contract_cols(activated, downward_weight[layer_index])
         saved.append(
             (
+                stream,
                 normed,
-                scaled,
-                rscale,
                 queries,
                 key_rows,
                 values,
                 probs,
                 probs_low,
                 context_flat,
-                scaled_mid,
-                rscale_mid,
+                mid_stream,
                 normed_mid,
                 preact,
                 activated,
             )
         )
-        ffn_sum = lax.psum(partial_ffn.astype(jnp.bfloat16), "mp").astype(jnp.float32)
-        stream = (mid_stream.astype(jnp.float32) + ffn_sum).astype(jnp.bfloat16)
-        normed, scaled, rscale = normalize(stream)
-        final_stream = stream
+        stream = summed(forward_sum, 0, n, partial_ffn.astype(jnp.bfloat16), mid_stream)
+    final_stream = stream
     gradients = []
     upstream = cotangent
     for layer_index in reversed(range(LAYERS)):
         (
+            stream,
             normed,
-            scaled,
-            rscale,
             queries,
             key_rows,
             values,
             probs,
             probs_low,
             context_flat,
-            scaled_mid,
-            rscale_mid,
+            mid_stream,
             normed_mid,
             preact,
             activated,
@@ -144,12 +267,14 @@
         _, gate_back = jax.vjp(smooth_gate, preact)
         grad_preact = gate_back(grad_act.astype(jnp.float32))[0].astype(jnp.bfloat16)
         upward_grad = contract_rows(normed_mid, grad_preact)
-        grad_normed = lax.psum(
-            contract_cols(grad_preact, upward_weight[layer_index]).astype(jnp.bfloat16), "mp"
-        ).astype(jnp.float32)
-        grad_mid = (
-            upstream.astype(jnp.float32) + norm_backward(scaled_mid, rscale_mid, grad_normed)
-        ).astype(jnp.bfloat16)
+        grad_mid = summed(
+            backward_sum,
+            1,
+            n,
+            contract_cols(grad_preact, upward_weight[layer_index]).astype(jnp.bfloat16),
+            mid_stream,
+            upstream,
+        )
         output_grad = contract_rows(grad_mid, context_flat)
         grad_context = jnp.dot(
             grad_mid, output_weight[layer_index], preferred_element_type=jnp.float32
@@ -163,38 +288,28 @@
             grad_context.reshape(slates, SLATE, heads_here, HD),
         )
         grad_qkv = jnp.stack([grad_query, grad_key, grad_value], axis=2).reshape(row_count, -1)
-        triple_grad = contract_rows(normed, grad_qkv).reshape(model_width, 3, -1)
+        triple_grad = contract_rows(normed, grad_qkv)
         pieces = (triple_grad, output_grad, upward_grad, downward_grad)
-        gradients.insert(0, pieces)
+        joined = jnp.concatenate([piece.astype(jnp.bfloat16) for piece in pieces], axis=1)
+        shares = lax.psum_scatter(joined, "dp", scatter_dimension=0, tiled=True)
+        cuts = [sum(piece.shape[1] for piece in pieces[:count]) for count in (1, 2, 3)]
+        gradients.insert(0, jnp.split(shares, cuts, axis=1))
         if layer_index > 0:
             flat_triple = triple_weight[layer_index].reshape(model_width, -1)
-            grad_input = lax.psum(
-                contract_cols(grad_qkv, flat_triple).astype(jnp.bfloat16), "mp"
-            ).astype(jnp.float32)
-            upstream = (
-                grad_mid.astype(jnp.float32) + norm_backward(scaled, rscale, grad_input)
-            ).astype(jnp.bfloat16)
-    stacked = tuple(
-        (
-            jnp.stack([gradients[layer_pos][slot_index] for layer_pos in range(LAYERS)])
-            for slot_index in range(4)
-        )
-    )
-    merged = (
-        lax.psum_scatter(
-            stacked[0].astype(jnp.bfloat16), "dp", scatter_dimension=1, tiled=True
-        ).astype(jnp.float32),
-        lax.psum_scatter(
-            stacked[1].astype(jnp.bfloat16), "dp", scatter_dimension=1, tiled=True
-        ).astype(jnp.float32),
-        lax.psum_scatter(
-            stacked[2].astype(jnp.bfloat16), "dp", scatter_dimension=1, tiled=True
-        ).astype(jnp.float32),
-        lax.psum_scatter(
-            stacked[3].astype(jnp.bfloat16), "dp", scatter_dimension=1, tiled=True
-        ).astype(jnp.float32),
-    )
-    return (final_stream, merged[0], merged[1], merged[2], merged[3])
+            upstream = summed(
+                backward_sum,
+                1,
+                n,
+                contract_cols(grad_qkv, flat_triple).astype(jnp.bfloat16),
+                stream,
+                grad_mid,
+            )
+    merged = [
+        jnp.stack([gradients[layer_pos][slot_index] for layer_pos in range(LAYERS)]).astype(jnp.float32)
+        for slot_index in range(4)
+    ]
+    triple = merged[0].reshape(LAYERS, merged[0].shape[1], 3, -1)
+    return (final_stream, triple, merged[1], merged[2], merged[3])
 
 
 def solution(mesh):
@@ -208,7 +323,7 @@
         P(None, None, "mp"),
     )
     return jax.shard_map(
-        body,
+        functools.partial(body, mesh.shape["mp"]),
         mesh=mesh,
         in_specs=placed,
         out_specs=(

time: 628 us -> 281 us (0.45)
  waiting for transfers between devices: 532 us -> 50.3 us
  Pallas kernels: 0 us -> 157 us
  other arithmetic: 29 us -> 8.27 us
  matrix products: 39.6 us -> 31.7 us
  local copies, waits for them, and re-layouts: 10 us -> 17.3 us
    psum x6 -> x0, waiting for transfers between devices: 434 us -> none  [the longest x2 147 us: body(): lax.psum(partial_att.astype(jnp.bfloat16), 'mp').astype(jnp.float32)]
    pallas_call x0 -> x7, Pallas kernels: none -> 157 us  [summed(): pl.pallas_call(functools.partial(kernel, n), out_shape=jax.ShapeDtypeStru...]
    reduce_scatter x4 -> x2, waiting for transfers between devices: 97 us -> 50.2 us  [body(): shares = lax.psum_scatter(joined, 'dp', scatter_dimension=0, tiled=True)]
    convert_element_type x8, other arithmetic: 13.3 us -> 1.87 us  [the longest x3 1.1 us: body(): jnp.stack([gradients[layer_pos][slot_index] for layer_pos in range(LAYERS)])]
  transfers between devices with their start and end apart: 10 -> 2, of which waited for: 10 -> 2; matrix products, arithmetic and copies ran while one was open for 4% -> 2% of each run, Pallas kernels for 0% -> 7%
where the time goes in v1:
time: 281 us; the launch traced here: 280 us
  Pallas kernels  157 us (56%)
  waiting for transfers between devices  50.3 us (18%)
  matrix products  31.7 us (11%)
  local copies, waits for them, and re-layouts  17.3 us (6%)
  between operations  15.4 us (5%)
  other arithmetic  8.27 us (3%)
    pallas_call x7, Pallas kernels, summed(): pl.pallas_call(functools.partial(kernel, n), out_shape=jax.ShapeDtypeStru...  157 us
    reduce_scatter x2, waiting for transfers between devices, body(): shares = lax.psum_scatter(joined, 'dp', scatter_dimension=0, tiled=True)  50.2 us
    unnamed x72, local copies, waits for them, and re-layouts  10.5 us
  transfers between devices with their start and end apart: 2, of which 2 were waited for; matrix products, arithmetic and copies ran while one was open for 2% of the time, Pallas kernels for 7%

profile of v1, /device:TPU:0, one launch (start us, length us, event | category | flops | bytes accessed | tf_op | source)
XLA Modules:
  0.0 280.0 jit_solution(12413705552839131065)
XLA Ops:
  7.2 2.4 fusion.109
  12.6 25.4 %shard_map.110.stream = bf16[8,32,1024]{2,1,0:T(8,128)(2,1)S(1)} custom-call(bf16[8,32,1024]{2,1,0:T(8,128)(2,1)S(1)} %bitcast.208, bf16[8,32,1024]{2,1,0:T(8,128)(2,1)S(1)} %bitcast.204), custom_call_target="tpu_custom_call" | custom-call | tf_op jit(solution)/shard_map/pallas_call | solution.py:186
  39.7 22.4 %shard_map.111.stream = bf16[8,32,1024]{2,1,0:T(8,128)(2,1)S(1)} custom-call(bf16[8,32,1024]{2,1,0:T(8,128)(2,1)S(1)} %bitcast.214, bf16[8,32,1024]{2,1,0:T(8,128)(2,1)S(1)} %shard_map.110.stream), custom_call_target="tpu_custom_call" | custom-call | tf_op jit(solution)/shard_map/pallas_call | solution.py:186
  62.5 1.6 copy.57
  65.4 1.2 fusion.78
  66.6 1.2 convolution_convert_fusion.27
  67.9 1.4 convolution_convert_fusion.11
  69.3 22.7 %shard_map.112.stream = bf16[8,32,1024]{2,1,0:T(8,128)(2,1)S(1)} custom-call(bf16[8,32,1024]{2,1,0:T(8,128)(2,1)S(1)} %bitcast.209, bf16[8,32,1024]{2,1,0:T(8,128)(2,1)S(1)} %shard_map.111.stream), custom_call_target="tpu_custom_call" | custom-call | tf_op jit(solution)/shard_map/pallas_call | solution.py:186
  95.0 21.1 %shard_map.114.upstream = bf16[8,32,1024]{2,1,0:T(8,128)(2,1)S(1)} custom-call(bf16[8,32,1024]{2,1,0:T(8,128)(2,1)S(1)} %bitcast.216, bf16[8,32,1024]{2,1,0:T(8,128)(2,1)S(1)} %shard_map.112.stream, bf16[8,32,1024]{2,1,0:T(8,128)(2,1)S(1)} %bitcast.215), custom_call_target="tpu_custom_call" | custom-call | tf_op jit(solution)/shard_map/pallas_call | solution.py:186
  116.5 1.9 fusion.96
  118.4 2.5 fusion.17
  120.9 2.5 fusion.18
  123.4 1.4 fusion.19
  126.4 23.1 %shard_map.115.upstream = bf16[8,32,1024]{2,1,0:T(8,128)(2,1)S(1)} custom-call(bf16[8,32,1024]{2,1,0:T(8,128)(2,1)S(1)} %bitcast.210, bf16[8,32,1024]{2,1,0:T(8,128)(2,1)S(1)} %shard_map.111.stream, bf16[8,32,1024]{2,1,0:T(8,128)(2,1)S(1)} %shard_map.114.upstream), custom_call_target="tpu_custom_call" | custom-call | tf_op jit(solution)/shard_map/pallas_call | solution.py:186
  150.9 22.0 %shard_map.116 = bf16[8,32,1024]{2,1,0:T(8,128)(2,1)S(1)} custom-call(bf16[8,32,1024]{2,1,0:T(8,128)(2,1)S(1)} %bitcast.217, bf16[8,32,1024]{2,1,0:T(8,128)(2,1)S(1)} %shard_map.110.stream, bf16[8,32,1024]{2,1,0:T(8,128)(2,1)S(1)} %shard_map.115.upstream), custom_call_target="tpu_custom_call" | custom-call | tf_op jit(solution)/shard_map/pallas_call | solution.py:186
  173.2 1.1 fusion.95
  174.3 2.5 fusion.20
  176.8 2.5 fusion.21
  179.3 1.9 fusion.22
  181.5 1.6 convolution_convert_fusion.2
  183.1 0.9 pad_maximum_fusion.3
  185.4 1.9 pad_maximum_fusion
  189.8 1.9 pad_maximum_fusion.1
  191.8 1.7 copy-done.27
  194.1 20.2 %shard_map.113 = bf16[8,32,1024]{2,1,0:T(8,128)(2,1)S(1)} custom-call(bf16[8,32,1024]{2,1,0:T(8,128)(2,1)S(1)} %bitcast.213, bf16[8,32,1024]{2,1,0:T(8,128)(2,1)S(1)} %shard_map.112.stream), custom_call_target="tpu_custom_call" | custom-call | tf_op jit(solution)/shard_map/pallas_call | solution.py:186
  214.2 10.6 %reduce-scatter.3.cloned.1.call-done = bf16[256,1536]{0,1:T(8,128)(2,1)} async-done(((bf16[1024,1536]{0,1:T(8,128)(2,1)}), bf16[256,1536]{0,1:T(8,128)(2,1)}) %reduce-scatter.3.cloned.1.call-update) | async-done | bytes 786448 | tf_op jit(solution)/shard_map/reduce_scatter | solution.py:294
  224.9 1.1 slice_bitcast_fusion.1
  225.9 39.6 %reduce-scatter.5.cloned.1.call-done = bf16[256,1536]{0,1:T(8,128)(2,1)} async-done(((bf16[1024,1536]{0,1:T(8,128)(2,1)}), bf16[256,1536]{0,1:T(8,128)(2,1)}) %reduce-scatter.5.cloned.1.call-update) | async-done | bytes 786448 | tf_op jit(solution)/shard_map/reduce_scatter | solution.py:294
  265.5 1.1 slice_bitcast_fusion
  266.8 1.3 copy.46
  268.1 1.3 copy.47
  271.4 0.9 maximum_convert_fusion.2
  (124 shorter events, 19.5 us)
Async XLA Ops:
  7.2 2.7 copy-start
  7.2 217.7 %reduce-scatter.3.cloned.1.call-start = ((), (), s32[]{:S(2)}) async-start(), calls=%async_computation.2 | async-start | bytes 3932160 | tf_op jit(solution)/shard_map/reduce_scatter | solution.py:294
  9.9 2.1 copy-start.7
  10.8 27.6 %copy-start.15 = (bf16[256,384]{0,1:T(8,128)(2,1)}, bf16[256,384]{0,1:T(8,128)(2,1)S(1)}, u32[]{:S(2)}) copy-start(bf16[256,384]{0,1:T(8,128)(2,1)S(1)} %copy.32) | copy-start | bytes 589828
  11.8 27.1 %copy-start.5 = (f32[2,256,256]{1,2,0:T(8,128)}, f32[2,256,256]{1,2,0:T(8,128)S(1)}, u32[]{:S(2)}) copy-start(f32[2,256,256]{1,2,0:T(8,128)S(1)} %fusion.80) | copy-start | bytes 1572868
  11.8 26.6 %copy-start.21 = (bf16[2,1024,512]{2,1,0:T(8,128)(2,1)S(1)}, bf16[2,1024,512]{2,1,0:T(8,128)(2,1)}, u32[]{:S(2)}) copy-start(bf16[2,1024,512]{2,1,0:T(8,128)(2,1)} %param.12) | copy-start | bytes 6291460
  12.0 26.9 %copy-start.24 = (bf16[2,1024,512]{2,1,0:T(8,128)(2,1)S(1)}, bf16[2,1024,512]{2,1,0:T(8,128)(2,1)}, u32[]{:S(2)}) copy-start(bf16[2,1024,512]{2,1,0:T(8,128)(2,1)} %param.13) | copy-start | bytes 6291460
  62.5 5.4 %copy-start.3 = (bf16[8,32,1024]{2,1,0:T(8,128)(2,1)}, bf16[8,32,1024]{2,1,0:T(8,128)(2,1)S(1)}, u32[]{:S(2)}) copy-start(bf16[8,32,1024]{2,1,0:T(8,128)(2,1)S(1)} %fusion.26) | copy-start | bytes 1572868
  66.6 1.3 copy-start.6
  66.6 25.8 %copy-start.22 = (bf16[2,1024,512]{2,1,0:T(8,128)(2,1)S(1)}, bf16[2,1024,512]{2,1,0:T(8,128)(2,1)}, u32[]{:S(2)}) copy-start(bf16[2,1024,512]{2,1,0:T(8,128)(2,1)} %param.12) | copy-start | bytes 6291460
  67.9 25.8 %copy-start.1 = (bf16[256,1024]{1,0:T(8,128)(2,1)S(1)}, bf16[256,1024]{1,0:T(8,128)(2,1)}, u32[]{:S(2)}) copy-start(bf16[256,1024]{1,0:T(8,128)(2,1)} %param.9) | copy-start | bytes 1572868
  67.9 25.8 %copy-start.25 = (bf16[2,1024,512]{2,1,0:T(8,128)(2,1)S(1)}, bf16[2,1024,512]{2,1,0:T(8,128)(2,1)}, u32[]{:S(2)}) copy-start(bf16[2,1024,512]{2,1,0:T(8,128)(2,1)} %param.13) | copy-start | bytes 6291460
  92.8 0.8 copy-start.28
  94.3 21.8 %copy-start.8 = (bf16[2,1024,128]{2,1,0:T(8,128)(2,1)S(1)}, bf16[2,1024,128]{2,1,0:T(8,128)(2,1)}, u32[]{:S(2)}) copy-start(bf16[2,1024,128]{2,1,0:T(8,128)(2,1)} %param.11) | copy-start | bytes 1572868
  123.4 26.1 %copy-start.26 = (bf16[2,1024,512]{2,1,0:T(8,128)(2,1)S(1)}, bf16[2,1024,512]{2,1,0:T(8,128)(2,1)}, u32[]{:S(2)}) copy-start(bf16[2,1024,512]{2,1,0:T(8,128)(2,1)} %param.13) | copy-start | bytes 6291460
  123.4 26.1 %copy-start.32 = (f32[256,512]{1,0:T(8,128)S(1)}, f32[256,512]{1,0:T(8,128)}, u32[]{:S(2)}) copy-start(f32[256,512]{1,0:T(8,128)} %copy-done.31) | copy-start | bytes 1572868
  126.4 23.8 %copy-start.23 = (bf16[2,1024,512]{2,1,0:T(8,128)(2,1)S(1)}, bf16[2,1024,512]{2,1,0:T(8,128)(2,1)}, u32[]{:S(2)}) copy-start(bf16[2,1024,512]{2,1,0:T(8,128)(2,1)} %param.12) | copy-start | bytes 6291460
  150.2 22.7 %copy-start.9 = (bf16[2,1024,128]{2,1,0:T(8,128)(2,1)S(1)}, bf16[2,1024,128]{2,1,0:T(8,128)(2,1)}, u32[]{:S(2)}) copy-start(bf16[2,1024,128]{2,1,0:T(8,128)(2,1)} %param.11) | copy-start | bytes 1572868
  150.2 23.0 %copy-start.16 = (bf16[256,384]{0,1:T(8,128)(2,1)S(1)}, bf16[256,384]{0,1:T(8,128)(2,1)}, u32[]{:S(2)}) copy-start(bf16[256,384]{0,1:T(8,128)(2,1)} %copy-done.15) | copy-start | bytes 589828
  150.9 30.3 %copy-start.14 = (bf16[2,64,256]{2,1,0:T(8,128)(2,1)S(1)}, bf16[2,64,256]{2,1,0:T(8,128)(2,1)}, u32[]{:S(2)}) copy-start(bf16[2,64,256]{2,1,0:T(8,128)(2,1)} %copy-done.13) | copy-start | bytes 196612
  181.4 3.2 %copy-start.20 = (bf16[256,512]{1,0:T(8,128)(2,1)S(1)}, bf16[256,512]{1,0:T(8,128)(2,1)}, u32[]{:S(2)}) copy-start(bf16[256,512]{1,0:T(8,128)(2,1)} %copy-done.19) | copy-start | bytes 786436
  187.3 1.0 copy-start.4
  187.3 1.1 copy-start.11
  187.3 1.5 copy-start.18
  187.3 1.9 copy-start.2
  187.3 1.9 copy-start.29
  187.4 78.2 %reduce-scatter.5.cloned.1.call-start = ((), (), s32[]{:S(2)}) async-start(), calls=%async_computation.3 | async-start | bytes 3932160 | tf_op jit(solution)/shard_map/reduce_scatter | solution.py:294
  191.8 1.7 copy-start.27
  191.8 1.8 copy-start.30
  266.7 2.6 copy-start.12
  268.1 3.0 %slice-start = ((bf16[256,1536]{0,1:T(8,128)(2,1)}), bf16[256,384]{0,1:T(8,128)(2,1)S(1)}, s32[]{:S(2)}) async-start(bf16[256,1536]{0,1:T(8,128)(2,1)} %reduce-scatter.3.cloned.1.call-done), calls=%async_computation.4 | async-start | bytes 393216 | tf_op jit(solution)/shard_map/split | solution.py:296
  268.1 3.2 %slice-start.1 = ((bf16[256,1536]{0,1:T(8,128)(2,1)}), bf16[256,384]{0,1:T(8,128)(2,1)S(1)}, s32[]{:S(2)}) async-start(bf16[256,1536]{0,1:T(8,128)(2,1)} %reduce-scatter.5.cloned.1.call-done), calls=%async_computation.5 | async-start | bytes 393216 | tf_op jit(solution)/shard_map/split | solution.py:296
  (5 other events, 3.5 us)
Sparse Core Ops, SparseCore 0:
  187.4 37.3 reduce-scatter.2
  227.5 37.9 reduce-scatter.4

commit v2 on v0

v2 whole, which is shorter than its diff:
```python
import functools

import jax
import jax.numpy as jnp
from jax import lax
from jax.experimental import pallas as pl
from jax.experimental.pallas import tpu as pltpu
from jax.sharding import PartitionSpec as P

HD = 64
SLATE = 256
LAYERS = 2
MESH = pl.DeviceIdType.MESH


epsilon = 1e-06


def normalize(stream):
    widened = stream.astype(jnp.float32)
    rscale = lax.rsqrt(jnp.mean(widened * widened, axis=-1, keepdims=True) + epsilon)
    scaled = widened * rscale
    return (scaled.astype(jnp.bfloat16), scaled, rscale)


def norm_backward(scaled, rscale, upward):
    inner = jnp.mean(upward * scaled, axis=-1, keepdims=True)
    return rscale * (upward - scaled * inner)


def contract_rows(left, right):
    return lax.dot_general(
        left, right, (((0,), (0,)), ((), ())), preferred_element_type=jnp.float32
    )


def contract_cols(left, right):
    return lax.dot_general(
        left, right, (((1,), (1,)), ((), ())), preferred_element_type=jnp.float32
    )


def remote(src, dst, send_sem, recv_sem, axis, device):
    return pltpu.make_async_remote_copy(
        src_ref=src,
        dst_ref=dst,
        send_sem=send_sem,
        recv_sem=recv_sem,
        device_id={axis: device},
        device_id_type=MESH,
    )


def place(axis, n):
    me = lax.axis_index(axis)
    parity = lax.rem(me, 2)
    group = lax.div(me, 2)
    partner = me + 1 - 2 * parity
    groups = n // 2
    return me, parity, group, partner, groups


ROOT = (2.0 / 3.141592653589793) ** 0.5
CUBIC = 0.044715


def gate(preact):
    bent = jnp.tanh(ROOT * (preact + CUBIC * (preact * preact * preact)))
    return 0.5 * preact * (1.0 + bent)


def gate_slope(preact):
    square = preact * preact
    bent = jnp.tanh(ROOT * (preact + CUBIC * (square * preact)))
    inner = ROOT * (1.0 + 3.0 * CUBIC * square)
    return 0.5 * (1.0 + bent) + 0.5 * preact * (1.0 - bent * bent) * inner


def dot(left, right):
    return jnp.dot(left, right, preferred_element_type=jnp.float32)


def low(value):
    return value.astype(jnp.bfloat16)


def wide(value):
    return value.astype(jnp.float32)


class Scatter:
    def __init__(self, axis, n, part, first, held, second, sems):
        self.axis, self.n = axis, n
        self.part, self.first, self.held, self.second, self.sems = part, first, held, second, sems
        self.me, self.parity, self.group, self.partner, self.groups = place(axis, n)
        self.order = list(range(1, self.groups)) + [0]
        self.copies = []

    def peer(self, j):
        return lax.rem(self.group + j, self.groups) * 2 + self.parity

    def start(self):
        self.to_pair = [None] * self.groups
        for j in self.order:
            theirs = lax.rem(self.group + j, self.groups) * 2 + 1 - self.parity
            self.to_pair[j] = remote(
                self.part.at[theirs],
                self.first.at[j],
                self.sems.at[0, j],
                self.sems.at[1, j],
                self.axis,
                self.partner,
            )
            self.to_pair[j].start()
        self.copies += self.to_pair

    def pass_on(self):
        self.to_peer = []
        for j in self.order[:-1]:
            peer = self.peer(j)
            self.to_pair[j].wait_recv()
            self.held[j] = low(wide(self.part[peer]) + wide(self.first[j]))
            copy = remote(
                self.held.at[j],
                self.second.at[j],
                self.sems.at[2, j],
                self.sems.at[3, j],
                self.axis,
                peer,
            )
            copy.start()
            self.to_peer.append(copy)
        self.copies += self.to_peer

    def total(self):
        self.to_pair[0].wait_recv()
        total = wide(self.part[self.me]) + wide(self.first[0])
        for j in self.order[:-1]:
            self.to_peer[j - 1].wait_recv()
            total = total + wide(self.second[j])
        return total

    def drain(self):
        for copy in self.copies:
            copy.wait_send()


class Reduce(Scatter):
    def __init__(self, axis, n, part, first, held, second, whole, sems):
        super().__init__(axis, n, part, first, held, second, sems)
        self.whole = whole

    def gather(self):
        mine = self.whole.at[self.me]
        self.around = []
        for j in range(1, self.groups):
            self.around.append(
                remote(mine, mine, self.sems.at[4, j], self.sems.at[5, j], self.axis, self.peer(j))
            )
            self.around[-1].start()
        across = remote(mine, mine, self.sems.at[6, 0], self.sems.at[7, 0], self.axis, self.partner)
        across.start()
        self.across = [across]

    def forward(self):
        for j in range(1, self.groups):
            self.around[j - 1].wait_recv()
            owner = lax.rem(self.group + self.groups - j, self.groups) * 2 + self.parity
            block = self.whole.at[owner]
            copy = remote(
                block, block, self.sems.at[6, j], self.sems.at[7, j], self.axis, self.partner
            )
            copy.start()
            self.across.append(copy)

    def finish(self):
        for copy in self.across:
            copy.wait_recv()
        self.copies += self.around + self.across


def greet(axes):
    barrier = pltpu.get_barrier_semaphore()
    count = 0
    for axis, n in axes:
        _, parity, group, partner, groups = place(axis, n)
        others = [partner]
        for j in range(1, groups):
            others.append(lax.rem(group + j, groups) * 2 + parity)
        for other in others:
            pl.semaphore_signal(barrier, inc=1, device_id={axis: other}, device_id_type=MESH)
        count += len(others)
    pl.semaphore_wait(barrier, count)


def kernel(
    n,
    m,
    lengths,
    tokens,
    cotangent,
    triple_weight,
    output_weight,
    upward_weight,
    downward_weight,
    final_out,
    triple_out,
    output_out,
    upward_out,
    downward_out,
    part,
    first,
    held,
    second,
    whole,
    sems,
    ffn_part,
    ffn_first,
    ffn_held,
    ffn_second,
    ffn_sems,
    out_part,
    out_first,
    out_held,
    out_second,
    out_sems,
    qkv_part,
    qkv_first,
    qkv_held,
    qkv_second,
    qkv_sems,
    normed,
    qkv,
    probs,
    context,
    normed_mid,
    slope,
    activated,
    grad_act,
    grad_qkv,
):
    greet((("mp", n), ("dp", m)))
    _, chunk, width = tokens.shape
    row_count = n * chunk
    slates = row_count // SLATE
    held_cols = output_weight.shape[-1]
    heads = held_cols // HD
    hidden = upward_weight.shape[-1]
    me = lax.axis_index("mp")
    position = lax.broadcasted_iota(jnp.int32, (1, SLATE), 1)

    def rows(ref):
        return ref[...].reshape(row_count, width)

    def reducer(k):
        return Reduce(
            "mp", n, part.at[k], first.at[k], held.at[k], second.at[k], whole.at[k], sems.at[k]
        )

    def put(k, value):
        part[k] = low(value).reshape(n, chunk, width)

    def scatterer(refs, l):
        return Scatter("dp", m, *[ref.at[l] for ref in refs])

    def put_grad(ref, l, start, value):
        columns = value.shape[1]
        ref[l, :, :, start : start + columns] = low(value).reshape(m, -1, columns)

    def slices(s, h):
        block = slice(s * SLATE, (s + 1) * SLATE)
        return block, [slice(i * held_cols + h * HD, i * held_cols + (h + 1) * HD) for i in range(3)]

    drained = []
    stream = tokens
    streams, mids = [], []
    for l in range(LAYERS):
        last = l == LAYERS - 1
        streams.append(stream)
        normed[l] = normalize(rows(stream))[0]
        qkv[l] = low(dot(normed[l], triple_weight[l]))
        for s in range(slates):
            live = wide(position < lengths[s])
            for h in range(heads):
                block, (q, k, v) = slices(s, h)
                scores = contract_cols(qkv[l, block, q], qkv[l, block, k]) * HD ** (-0.5)
                weights = jnp.exp(scores) * live
                share = weights / jnp.sum(weights, axis=-1, keepdims=True)
                probs[l, s * heads + h] = share
                context[l, block, h * HD : (h + 1) * HD] = low(dot(low(share), qkv[l, block, v]))
        step = reducer(2 * l)
        put(2 * l, contract_cols(context[l], output_weight[l]))
        step.start()
        if l == 0:
            grad_act[...] = low(dot(rows(cotangent), downward_weight[LAYERS - 1]))
        step.pass_on()
        whole[2 * l, me] = low(wide(stream[me]) + step.total())
        step.gather()
        step.forward()
        step.finish()
        drained.append(step)
        mid = whole.at[2 * l]
        mids.append(mid)
        normed_mid[l] = normalize(rows(mid))[0]
        preact = dot(normed_mid[l], upward_weight[l])
        activated[l] = low(gate(preact))
        if not last:
            put(2 * l + 1, contract_cols(activated[l], downward_weight[l]))
            step = reducer(2 * l + 1)
            step.start()
            slope[l] = gate_slope(preact)
            step.pass_on()
            whole[2 * l + 1, me] = low(wide(mid[me]) + step.total())
            step.gather()
            step.forward()
            step.finish()
            drained.append(step)
            stream = whole.at[2 * l + 1]
        else:
            slope[l] = gate_slope(preact)

    final_k = 2 * LAYERS - 1
    final = reducer(final_k)

    def final_gather():
        whole[final_k, me] = low(wide(mids[-1][me]) + final.total())
        final.gather()

    def final_finish():
        final.finish()
        final_out[...] = whole[final_k]

    later = [final.start, final.pass_on, final_gather, final.forward, final_finish]

    def advance():
        if later:
            later.pop(0)()

    pending = []

    def flush():
        while pending:
            pending.pop(0)()

    def ffn_done(scatter, l):
        total = scatter.total()
        downward_out[l] = total[:, :hidden]
        upward_out[l] = total[:, hidden:]

    def out_done(scatter, l):
        output_out[l] = scatter.total()

    def qkv_done(scatter, l):
        triple_out[l] = scatter.total()

    upstream = cotangent
    k_next = 2 * LAYERS
    for l in reversed(range(LAYERS)):
        if l == LAYERS - 1:
            act_back = grad_act[...]
        else:
            act_back = low(dot(rows(upstream), downward_weight[l]))
        grad_preact = low(wide(act_back) * slope[l])
        step = reducer(k_next)
        put(k_next, contract_cols(grad_preact, upward_weight[l]))
        step.start()
        ffn = scatterer((ffn_part, ffn_first, ffn_held, ffn_second, ffn_sems), l)
        put_grad(ffn_part, l, 0, contract_rows(rows(upstream), activated[l]))
        step.pass_on()
        put_grad(ffn_part, l, hidden, contract_rows(normed_mid[l], grad_preact))
        ffn.start()
        if l == LAYERS - 1:
            put(final_k, contract_cols(activated[l], downward_weight[l]))
        _, scaled, rscale = normalize(mids[l][me])
        whole[k_next, me] = low(wide(upstream[me]) + norm_backward(scaled, rscale, step.total()))
        step.gather()
        flush()
        ffn.pass_on()
        step.forward()
        step.finish()
        advance()
        drained += [step, ffn]
        grad_mid = whole.at[k_next]
        k_next += 1
        put_grad(out_part, l, 0, contract_rows(rows(grad_mid), context[l]))
        out = scatterer((out_part, out_first, out_held, out_second, out_sems), l)
        out.start()
        grad_context = low(dot(rows(grad_mid), output_weight[l]))
        for s in range(slates):
            for h in range(heads):
                block, (q, k, v) = slices(s, h)
                share = probs[l, s * heads + h]
                back = grad_context[block, h * HD : (h + 1) * HD]
                grad_prob = contract_cols(back, qkv[l, block, v])
                grad_qkv[l, block, v] = low(contract_rows(low(share), back))
                inner = jnp.sum(grad_prob * share, axis=-1, keepdims=True)
                grad_score = low(share * (grad_prob - inner) * HD ** (-0.5))
                grad_qkv[l, block, q] = low(dot(grad_score, qkv[l, block, k]))
                grad_qkv[l, block, k] = low(contract_rows(grad_score, qkv[l, block, q]))
        triple = scatterer((qkv_part, qkv_first, qkv_held, qkv_second, qkv_sems), l)
        drained += [out, triple]
        if l > 0:
            step = reducer(k_next)
            put(k_next, contract_cols(grad_qkv[l], triple_weight[l]))
            step.start()
            out.pass_on()
            put_grad(qkv_part, l, 0, contract_rows(normed[l], grad_qkv[l]))
            step.pass_on()
            triple.start()
            _, scaled, rscale = normalize(streams[l][me])
            whole[k_next, me] = low(
                wide(grad_mid[me]) + norm_backward(scaled, rscale, step.total())
            )
            step.gather()
            ffn_done(ffn, l)
            triple.pass_on()
            step.forward()
            step.finish()
            advance()
            drained.append(step)
            upstream = whole.at[k_next]
            k_next += 1
            pending.append(functools.partial(out_done, out, l))
            pending.append(functools.partial(qkv_done, triple, l))
        else:
            put_grad(qkv_part, l, 0, contract_rows(normed[l], grad_qkv[l]))
            triple.start()
            out.pass_on()
            advance()
            triple.pass_on()
            advance()
            ffn_done(ffn, l)
            out_done(out, l)
            while later:
                advance()
            qkv_done(triple, l)
    drained.append(final)
    for item in drained:
        item.drain()


def body(
    n, m, tokens, lengths, cotangent, triple_weight, output_weight, upward_weight, downward_weight
):
    row_count, width = tokens.shape
    chunk = row_count // n
    share = width // m
    held_cols = output_weight.shape[-1]
    hidden = upward_weight.shape[-1]
    triple_cols = 3 * held_cols
    heads_all = (row_count // SLATE) * (held_cols // HD)
    sums = 2 * LAYERS + 2 * LAYERS - 1
    vmem = pl.BlockSpec(memory_space=pltpu.VMEM)
    smem = pl.BlockSpec(memory_space=pltpu.SMEM)
    bf16, f32 = jnp.bfloat16, jnp.float32

    def scratch(count, parts, rows, columns):
        half = pltpu.VMEM((count, parts // 2, rows, columns), bf16)
        return [pltpu.VMEM((count, parts, rows, columns), bf16), half, half, half]

    def sems(count, kinds, parts):
        return pltpu.SemaphoreType.DMA((count, kinds, parts // 2))

    outs = pl.pallas_call(
        functools.partial(kernel, n, m),
        out_shape=[
            jax.ShapeDtypeStruct((n, chunk, width), bf16),
            jax.ShapeDtypeStruct((LAYERS, share, triple_cols), f32),
            jax.ShapeDtypeStruct((LAYERS, share, held_cols), f32),
            jax.ShapeDtypeStruct((LAYERS, share, hidden), f32),
            jax.ShapeDtypeStruct((LAYERS, share, hidden), f32),
        ],
        in_specs=[smem] + [vmem] * 6,
        out_specs=[vmem] * 5,
        scratch_shapes=scratch(sums, n, chunk, width)
        + [pltpu.VMEM((sums, n, chunk, width), bf16), sems(sums, 8, n)]
        + scratch(LAYERS, m, share, 2 * hidden)
        + [sems(LAYERS, 4, m)]
        + scratch(LAYERS, m, share, held_cols)
        + [sems(LAYERS, 4, m)]
        + scratch(LAYERS, m, share, triple_cols)
        + [sems(LAYERS, 4, m)]
        + [
            pltpu.VMEM((LAYERS, row_count, width), bf16),
            pltpu.VMEM((LAYERS, row_count, triple_cols), bf16),
            pltpu.VMEM((LAYERS, heads_all, SLATE, SLATE), f32),
            pltpu.VMEM((LAYERS, row_count, held_cols), bf16),
            pltpu.VMEM((LAYERS, row_count, width), bf16),
            pltpu.VMEM((LAYERS, row_count, hidden), f32),
            pltpu.VMEM((LAYERS, row_count, hidden), bf16),
            pltpu.VMEM((row_count, hidden), bf16),
            pltpu.VMEM((LAYERS, row_count, triple_cols), bf16),
        ],
        compiler_params=pltpu.CompilerParams(
            collective_id=0, has_side_effects=True, vmem_limit_bytes=58 << 20
        ),
    )(
        lengths,
        tokens.reshape(n, chunk, width),
        cotangent.reshape(n, chunk, width),
        triple_weight.reshape(LAYERS, width, triple_cols),
        output_weight,
        upward_weight,
        downward_weight,
    )
    final, triple, output, upward, downward = outs
    return (
        final.reshape(row_count, width),
        triple.reshape(LAYERS, share, 3, held_cols),
        output,
        upward,
        downward,
    )


def solution(mesh):
    placed = (
        P("dp", None),
        P("dp"),
        P("dp", None),
        P(None, None, None, "mp"),
        P(None, None, "mp"),
        P(None, None, "mp"),
        P(None, None, "mp"),
    )
    return jax.shard_map(
        functools.partial(body, mesh.shape["mp"], mesh.shape["dp"]),
        mesh=mesh,
        in_specs=placed,
        out_specs=(
            P("dp", None),
            P(None, "dp", None, "mp"),
            P(None, "dp", "mp"),
            P(None, "dp", "mp"),
            P(None, "dp", "mp"),
        ),
        check_vma=False,
    )
```

time: 628 us -> 166 us (0.26)
  waiting for transfers between devices: 532 us -> 0 us
  Pallas kernels: 0 us -> 155 us
  matrix products: 39.6 us -> 0 us
  other arithmetic: 29 us -> 0 us
  between operations: 15.2 us -> 1.33 us
    psum x6 -> x0, waiting for transfers between devices: 434 us -> none  [the longest x2 147 us: body(): lax.psum(partial_att.astype(jnp.bfloat16), 'mp').astype(jnp.float32)]
    pallas_call x0 -> x1, Pallas kernels: none -> 155 us  [body(): pl.pallas_call(functools.partial(kernel, n, m), out_shape=[jax.ShapeDtype...]
    reduce_scatter x4 -> x0, waiting for transfers between devices: 97 us -> none  [the longest x1 32.1 us: body(): lax.psum_scatter(stacked[2].astype(jnp.bfloat16), 'dp', scatter_dimension...]
    dot_general x33 -> x0, matrix products: 38 us -> none  [the longest x7 9.97 us: contract_cols(): lax.dot_general(left, right, (((1,), (1,)), ((), ())), preferred_element_...]
    convert_element_type x9 -> x0, other arithmetic: 13.3 us -> none  [the longest x4 7.84 us: body(): merged = (lax.psum_scatter(stacked[0].astype(jnp.bfloat16), 'dp', scatter...]
    reduce_sum x7 -> x0, other arithmetic: 8.66 us -> none  [the longest x4 4.4 us: normalize(): jnp.mean(widened * widened, axis=-1, keepdims=True) + epsilon]
    another operation x6 -> x0, other arithmetic: 6.97 us -> none  [the longest x4 5.16 us: body(): jnp.stack([gradients[layer_pos][slot_index] for layer_pos in range(LAYERS)])]
  transfers between devices with their start and end apart: 10 -> 0, of which waited for: 10 -> 0; matrix products, arithmetic and copies ran while one was open for 4% -> 0% of each run, Pallas kernels for 0% -> 0%
where the time goes in v2:
time: 166 us
  Pallas kernels  155 us (93%)
  local copies, waits for them, and re-layouts  9.36 us (6%)
    pallas_call x1, Pallas kernels, body(): pl.pallas_call(functools.partial(kernel, n, m), out_shape=[jax.ShapeDtype...  155 us
    unnamed x14, local copies, waits for them, and re-layouts  6.31 us

profile of v2, /device:TPU:0, one launch (start us, length us, event | category | flops | bytes accessed | tf_op | source)
XLA Modules:
  0.0 166.0 jit_solution(16739254329213755282)
XLA Ops:
  1.3 1.7 %copy.14 = bf16[2,1024,3,128]{1,3,2,0:T(8,128)(2,1)S(1)} copy(bf16[2,1024,3,128]{3,1,2,0:T(8,128)(2,1)} %param.10) | data formatting | bytes 3145728 | tf_op args[3]
  3.0 1.6 copy.15.triple_weight
  4.6 155.3 %shard_map.110 = (bf16[8,32,1024]{2,1,0:T(8,128)(2,1)}, f32[2,256,384]{2,1,0:T(8,128)}, f32[2,256,128]{2,1,0:T(8,128)}, f32[2,256,512]{2,1,0:T(8,128)}, f32[2,256,512]{2,1,0:T(8,128)}) custom-call(s32[1]{0:T(128)S(6)} %copy.22.lengths, bf16[8,32,1024]{2,1,0:T(8,128)(2,1)} %bitcast.8, bf16[8,32,1024]{2,1,0:T(8,128)(2,1)} %bitcast.9, ...), custom_call_target="tpu_custom_call" | custom-call | tf_op jit(solution)/shard_map/pallas_call | solution.py:464
  159.9 0.0 copy-start.2
  159.9 1.5 copy.16
  161.3 0.0 copy-start.3
  161.3 0.0 copy-start.1
  161.4 1.1 copy.17
  162.5 0.0 copy-done.2
  162.5 0.8 copy.23
  163.3 0.0 copy-done.3
  163.3 0.0 copy-start
  163.3 0.7 copy.24
  164.0 0.0 copy-done.1
  164.0 1.0 copy.25
  165.0 0.0 copy-done
  165.0 1.0 copy.26
Async XLA Ops:
  159.9 2.6 %copy-start.2 = (bf16[8,32,1024]{2,1,0:T(8,128)(2,1)S(1)}, bf16[8,32,1024]{2,1,0:T(8,128)(2,1)}, u32[]{:S(2)}) copy-start(bf16[8,32,1024]{2,1,0:T(8,128)(2,1)} %get-tuple-element.10) | copy-start | bytes 1572868
  161.3 2.0 %copy-start.3 = (f32[2,256,128]{2,1,0:T(8,128)S(1)}, f32[2,256,128]{2,1,0:T(8,128)}, u32[]{:S(2)}) copy-start(f32[2,256,128]{2,1,0:T(8,128)} %get-tuple-element.32) | copy-start | bytes 786436
  161.3 2.7 %copy-start.1 = (f32[2,256,512]{2,1,0:T(8,128)S(1)}, f32[2,256,512]{2,1,0:T(8,128)}, u32[]{:S(2)}) copy-start(f32[2,256,512]{2,1,0:T(8,128)} %get-tuple-element.33) | copy-start | bytes 3145732
  163.3 1.7 %copy-start = (f32[2,256,512]{2,1,0:T(8,128)S(1)}, f32[2,256,512]{2,1,0:T(8,128)}, u32[]{:S(2)}) copy-start(f32[2,256,512]{2,1,0:T(8,128)} %get-tuple-element.34) | copy-start | bytes 3145732

commit v3 on v2

--- a/solution.py
+++ b/solution.py
@@ -199,31 +199,47 @@
     lengths,
     tokens,
     cotangent,
+    triple_hbm,
+    output_hbm,
+    upward_hbm,
+    downward_hbm,
+    final_hbm,
+    triple_out_hbm,
+    output_out_hbm,
+    upward_out_hbm,
+    downward_out_hbm,
     triple_weight,
     output_weight,
     upward_weight,
     downward_weight,
-    final_out,
     triple_out,
     output_out,
     upward_out,
     downward_out,
+    in_sems,
+    out_sems,
+    final_sem,
     part,
     first,
     held,
     second,
     whole,
     sems,
-    ffn_part,
-    ffn_first,
-    ffn_held,
-    ffn_second,
-    ffn_sems,
-    out_part,
-    out_first,
-    out_held,
-    out_second,
-    out_sems,
+    down_part,
+    down_first,
+    down_held,
+    down_second,
+    down_sems,
+    up_part,
+    up_first,
+    up_held,
+    up_second,
+    up_sems,
+    att_part,
+    att_first,
+    att_held,
+    att_second,
+    att_sems,
     qkv_part,
     qkv_first,
     qkv_held,
@@ -237,48 +253,102 @@
     slope,
     activated,
     grad_act,
+    grad_preact,
+    grad_context,
     grad_qkv,
 ):
+    pairs = (
+        (triple_hbm, triple_weight),
+        (output_hbm, output_weight),
+        (upward_hbm, upward_weight),
+        (downward_hbm, downward_weight),
+    )
+    loads = [
+        [pltpu.make_async_copy(far.at[l], near.at[l], in_sems.at[l, i]) for i, (far, near) in enumerate(pairs)]
+        for l in range(LAYERS)
+    ]
+    for layer_loads in loads:
+        for copy in layer_loads:
+            copy.start()
     greet((("mp", n), ("dp", m)))
-    _, chunk, width = tokens.shape
-    row_count = n * chunk
+    halves, _, chunk, width = tokens.shape
+    half_rows = n * chunk
+    row_count = halves * half_rows
     slates = row_count // SLATE
     held_cols = output_weight.shape[-1]
     heads = held_cols // HD
-    hidden = upward_weight.shape[-1]
     me = lax.axis_index("mp")
     position = lax.broadcasted_iota(jnp.int32, (1, SLATE), 1)
 
     def rows(ref):
         return ref[...].reshape(row_count, width)
 
-    def reducer(k):
-        return Reduce(
-            "mp", n, part.at[k], first.at[k], held.at[k], second.at[k], whole.at[k], sems.at[k]
-        )
-
-    def put(k, value):
-        part[k] = low(value).reshape(n, chunk, width)
+    def half(ref, a):
+        return ref[a].reshape(half_rows, width)
+
+    def cut(a):
+        return slice(a * half_rows, (a + 1) * half_rows)
+
+    def opened(k, a, value):
+        part[k, a] = low(value).reshape(n, chunk, width)
+        return reducer(k, a)
+
+    def reducer(k, a):
+        refs = [ref.at[k, a] for ref in (part, first, held, second, whole, sems)]
+        return Reduce("mp", n, *refs)
 
     def scatterer(refs, l):
         return Scatter("dp", m, *[ref.at[l] for ref in refs])
 
-    def put_grad(ref, l, start, value):
-        columns = value.shape[1]
-        ref[l, :, :, start : start + columns] = low(value).reshape(m, -1, columns)
+    def put_grad(ref, l, value):
+        ref[l] = low(value).reshape(m, -1, value.shape[1])
 
     def slices(s, h):
         block = slice(s * SLATE, (s + 1) * SLATE)
         return block, [slice(i * held_cols + h * HD, i * held_cols + (h + 1) * HD) for i in range(3)]
 
+    def joined(l):
+        return jnp.concatenate([triple_weight[l, i] for i in range(3)], axis=-1)
+
+    def nothing():
+        return None
+
     drained = []
+    span = range(halves)
+
+    def close(k, steps, own, first_work=nothing, second_work=nothing):
+        for step in steps:
+            step.pass_on()
+        first_work()
+        for a in span:
+            whole[k, a, me] = low(own(a, steps[a].total()))
+            steps[a].gather()
+        second_work()
+        for step in steps:
+            step.forward()
+        drained.extend(steps)
+
+    def added(stream):
+        return lambda a, total: wide(stream[a, me]) + total
+
+    def normed_back(stream, upstream):
+        def own(a, total):
+            _, scaled, rscale = normalize(stream[a, me])
+            return wide(upstream[a, me]) + norm_backward(scaled, rscale, total)
+
+        return own
+
     stream = tokens
+    arriving = None
     streams, mids = [], []
     for l in range(LAYERS):
-        last = l == LAYERS - 1
         streams.append(stream)
-        normed[l] = normalize(rows(stream))[0]
-        qkv[l] = low(dot(normed[l], triple_weight[l]))
+        loads[l][0].wait()
+        for a in span:
+            if arriving is not None:
+                arriving[a].finish()
+            normed[l, cut(a)] = normalize(half(stream, a))[0]
+            qkv[l, cut(a)] = low(dot(normed[l, cut(a)], joined(l)))
         for s in range(slates):
             live = wide(position < lengths[s])
             for h in range(heads):
@@ -288,104 +358,146 @@
                 share = weights / jnp.sum(weights, axis=-1, keepdims=True)
                 probs[l, s * heads + h] = share
                 context[l, block, h * HD : (h + 1) * HD] = low(dot(low(share), qkv[l, block, v]))
-        step = reducer(2 * l)
-        put(2 * l, contract_cols(context[l], output_weight[l]))
-        step.start()
-        if l == 0:
-            grad_act[...] = low(dot(rows(cotangent), downward_weight[LAYERS - 1]))
-        step.pass_on()
-        whole[2 * l, me] = low(wide(stream[me]) + step.total())
-        step.gather()
-        step.forward()
-        step.finish()
-        drained.append(step)
-        mid = whole.at[2 * l]
+        loads[l][1].wait()
+        k_here = 2 * l
+        steps = []
+        for a in span:
+            steps.append(opened(k_here, a, contract_cols(context[l, cut(a)], output_weight[l])))
+            steps[a].start()
+
+        def early(l=l):
+            loads[l][2].wait()
+            loads[l][3].wait()
+            if l == LAYERS - 1:
+                for a in span:
+                    grad_act[cut(a)] = low(dot(half(cotangent, a), downward_weight[l]))
+
+        close(k_here, steps, added(stream), early)
+        mid = whole.at[k_here]
         mids.append(mid)
-        normed_mid[l] = normalize(rows(mid))[0]
-        preact = dot(normed_mid[l], upward_weight[l])
-        activated[l] = low(gate(preact))
-        if not last:
-            put(2 * l + 1, contract_cols(activated[l], downward_weight[l]))
-            step = reducer(2 * l + 1)
-            step.start()
-            slope[l] = gate_slope(preact)
-            step.pass_on()
-            whole[2 * l + 1, me] = low(wide(mid[me]) + step.total())
-            step.gather()
-            step.forward()
-            step.finish()
-            drained.append(step)
-            stream = whole.at[2 * l + 1]
-        else:
-            slope[l] = gate_slope(preact)
+        if l == LAYERS - 1:
+            break
+        nexts = []
+        for a in span:
+            steps[a].finish()
+            normed_mid[l, cut(a)] = normalize(half(mid, a))[0]
+            preact = dot(normed_mid[l, cut(a)], upward_weight[l])
+            activated[l, cut(a)] = low(gate(preact))
+            nexts.append(
+                opened(k_here + 1, a, contract_cols(activated[l, cut(a)], downward_weight[l]))
+            )
+            nexts[a].start()
+            slope[l, cut(a)] = gate_slope(preact)
+        close(k_here + 1, nexts, added(mid))
+        stream = whole.at[k_here + 1]
+        arriving = nexts
 
     final_k = 2 * LAYERS - 1
-    final = reducer(final_k)
+    finals = [reducer(final_k, a) for a in span]
+    final_copy = pltpu.make_async_copy(whole.at[final_k], final_hbm, final_sem)
 
     def final_gather():
-        whole[final_k, me] = low(wide(mids[-1][me]) + final.total())
-        final.gather()
+        for a in span:
+            whole[final_k, a, me] = low(wide(mids[-1][a, me]) + finals[a].total())
+            finals[a].gather()
 
     def final_finish():
-        final.finish()
-        final_out[...] = whole[final_k]
-
-    later = [final.start, final.pass_on, final_gather, final.forward, final_finish]
+        for item in finals:
+            item.finish()
+        final_copy.start()
+
+    def each(name):
+        def act():
+            for item in finals:
+                getattr(item, name)()
+
+        return act
+
+    later = [each("start"), each("pass_on"), final_gather, each("forward"), final_finish]
 
     def advance():
         if later:
             later.pop(0)()
 
+    stores = [final_copy]
+
+    def store(i, l, near, far):
+        copy = pltpu.make_async_copy(near.at[l], far.at[l], out_sems.at[l, i])
+        copy.start()
+        stores.append(copy)
+
+    def triple_done(scatter, l):
+        total = scatter.total()
+        for i in range(3):
+            triple_out[l, i] = total[:, i * held_cols : (i + 1) * held_cols]
+        store(0, l, triple_out, triple_out_hbm)
+
+    def output_done(scatter, l):
+        output_out[l] = scatter.total()
+        store(1, l, output_out, output_out_hbm)
+
+    def upward_done(scatter, l):
+        upward_out[l] = scatter.total()
+        store(2, l, upward_out, upward_out_hbm)
+
+    def downward_done(scatter, l):
+        downward_out[l] = scatter.total()
+        store(3, l, downward_out, downward_out_hbm)
+
     pending = []
 
     def flush():
         while pending:
             pending.pop(0)()
 
-    def ffn_done(scatter, l):
-        total = scatter.total()
-        downward_out[l] = total[:, :hidden]
-        upward_out[l] = total[:, hidden:]
-
-    def out_done(scatter, l):
-        output_out[l] = scatter.total()
-
-    def qkv_done(scatter, l):
-        triple_out[l] = scatter.total()
-
     upstream = cotangent
+    arriving = steps
     k_next = 2 * LAYERS
     for l in reversed(range(LAYERS)):
-        if l == LAYERS - 1:
-            act_back = grad_act[...]
-        else:
-            act_back = low(dot(rows(upstream), downward_weight[l]))
-        grad_preact = low(wide(act_back) * slope[l])
-        step = reducer(k_next)
-        put(k_next, contract_cols(grad_preact, upward_weight[l]))
-        step.start()
-        ffn = scatterer((ffn_part, ffn_first, ffn_held, ffn_second, ffn_sems), l)
-        put_grad(ffn_part, l, 0, contract_rows(rows(upstream), activated[l]))
-        step.pass_on()
-        put_grad(ffn_part, l, hidden, contract_rows(normed_mid[l], grad_preact))
-        ffn.start()
-        if l == LAYERS - 1:
-            put(final_k, contract_cols(activated[l], downward_weight[l]))
-        _, scaled, rscale = normalize(mids[l][me])
-        whole[k_next, me] = low(wide(upstream[me]) + norm_backward(scaled, rscale, step.total()))
-        step.gather()
-        flush()
-        ffn.pass_on()
-        step.forward()
-        step.finish()
-        advance()
-        drained += [step, ffn]
+        last = l == LAYERS - 1
+        steps = []
+        for a in span:
+            arriving[a].finish()
+            if last:
+                normed_mid[l, cut(a)] = normalize(half(mids[l], a))[0]
+                preact = dot(normed_mid[l, cut(a)], upward_weight[l])
+                slope[l, cut(a)] = gate_slope(preact)
+                act_back = grad_act[cut(a)]
+            else:
+                act_back = low(dot(half(upstream, a), downward_weight[l]))
+            grad_preact[l, cut(a)] = low(wide(act_back) * slope[l, cut(a)])
+            steps.append(
+                opened(k_next, a, contract_cols(grad_preact[l, cut(a)], upward_weight[l]))
+            )
+            steps[a].start()
+            if last:
+                activated[l, cut(a)] = low(gate(preact))
+        down = scatterer((down_part, down_first, down_held, down_second, down_sems), l)
+        up = scatterer((up_part, up_first, up_held, up_second, up_sems), l)
+        att = scatterer((att_part, att_first, att_held, att_second, att_sems), l)
+        triple = scatterer((qkv_part, qkv_first, qkv_held, qkv_second, qkv_sems), l)
+        drained += [down, up, att, triple]
+
+        def feed_grads(l=l, down=down, up=up, upstream=upstream):
+            put_grad(down_part, l, contract_rows(rows(upstream), activated[l]))
+            down.start()
+            put_grad(up_part, l, contract_rows(normed_mid[l], grad_preact[l]))
+            up.start()
+
+        def feed_pass(l=l, down=down, up=up):
+            down.pass_on()
+            up.pass_on()
+            if l == LAYERS - 1:
+                for a in span:
+                    opened(final_k, a, contract_cols(activated[l, cut(a)], downward_weight[l]))
+
+        close(k_next, steps, normed_back(mids[l], upstream), feed_grads, feed_pass)
         grad_mid = whole.at[k_next]
         k_next += 1
-        put_grad(out_part, l, 0, contract_rows(rows(grad_mid), context[l]))
-        out = scatterer((out_part, out_first, out_held, out_second, out_sems), l)
-        out.start()
-        grad_context = low(dot(rows(grad_mid), output_weight[l]))
+        for a in span:
+            steps[a].finish()
+            grad_context[cut(a)] = low(dot(half(grad_mid, a), output_weight[l]))
+        advance()
         for s in range(slates):
             for h in range(heads):
                 block, (q, k, v) = slices(s, h)
@@ -397,53 +509,79 @@
                 grad_score = low(share * (grad_prob - inner) * HD ** (-0.5))
                 grad_qkv[l, block, q] = low(dot(grad_score, qkv[l, block, k]))
                 grad_qkv[l, block, k] = low(contract_rows(grad_score, qkv[l, block, q]))
-        triple = scatterer((qkv_part, qkv_first, qkv_held, qkv_second, qkv_sems), l)
-        drained += [out, triple]
+
+        def att_grad(l=l, grad_mid=grad_mid, att=att):
+            put_grad(att_part, l, contract_rows(rows(grad_mid), context[l]))
+            att.start()
+
+        def triple_grad(l=l, triple=triple):
+            put_grad(qkv_part, l, contract_rows(normed[l], grad_qkv[l]))
+            triple.start()
+
         if l > 0:
-            step = reducer(k_next)
-            put(k_next, contract_cols(grad_qkv[l], triple_weight[l]))
-            step.start()
-            out.pass_on()
-            put_grad(qkv_part, l, 0, contract_rows(normed[l], grad_qkv[l]))
-            step.pass_on()
-            triple.start()
-            _, scaled, rscale = normalize(streams[l][me])
-            whole[k_next, me] = low(
-                wide(grad_mid[me]) + norm_backward(scaled, rscale, step.total())
-            )
-            step.gather()
-            ffn_done(ffn, l)
-            triple.pass_on()
-            step.forward()
-            step.finish()
-            advance()
-            drained.append(step)
+            steps = []
+            for a in span:
+                steps.append(opened(k_next, a, contract_cols(grad_qkv[l, cut(a)], joined(l))))
+                steps[a].start()
+
+            def attend_grads(att_grad=att_grad, triple_grad=triple_grad):
+                att_grad()
+                triple_grad()
+
+            def attend_pass(att=att, triple=triple):
+                att.pass_on()
+                triple.pass_on()
+                advance()
+
+            close(k_next, steps, normed_back(streams[l], grad_mid), attend_grads, attend_pass)
+            arriving = steps
             upstream = whole.at[k_next]
             k_next += 1
-            pending.append(functools.partial(out_done, out, l))
-            pending.append(functools.partial(qkv_done, triple, l))
+            pending.append(functools.partial(downward_done, down, l))
+            pending.append(functools.partial(upward_done, up, l))
+            pending.append(functools.partial(output_done, att, l))
+            pending.append(functools.partial(triple_done, triple, l))
         else:
-            put_grad(qkv_part, l, 0, contract_rows(normed[l], grad_qkv[l]))
-            triple.start()
-            out.pass_on()
+            triple_grad()
+            att_grad()
             advance()
             triple.pass_on()
+            att.pass_on()
             advance()
-            ffn_done(ffn, l)
-            out_done(out, l)
+            flush()
+            downward_done(down, l)
+            upward_done(up, l)
             while later:
                 advance()
-            qkv_done(triple, l)
-    drained.append(final)
+            output_done(att, l)
+            triple_done(triple, l)
+    drained += finals
     for item in drained:
         item.drain()
+    for copy in stores:
+        copy.wait()
+
+
+def hand_over(*refs):
+    count = (len(refs) - 1) // 2
+    sems = refs[-1]
+    copies = [
+        pltpu.make_async_copy(refs[i].at[j], refs[count + i].at[j], sems.at[i, j])
+        for i in range(count)
+        for j in range(refs[i].shape[0])
+    ]
+    for copy in copies:
+        copy.start()
+    for copy in copies:
+        copy.wait()
 
 
 def body(
     n, m, tokens, lengths, cotangent, triple_weight, output_weight, upward_weight, downward_weight
 ):
     row_count, width = tokens.shape
-    chunk = row_count // n
+    halves = 2 if (row_count // n) % 32 == 0 else 1
+    chunk = row_count // (n * halves)
     share = width // m
     held_cols = output_weight.shape[-1]
     hidden = upward_weight.shape[-1]
@@ -452,34 +590,47 @@
     sums = 2 * LAYERS + 2 * LAYERS - 1
     vmem = pl.BlockSpec(memory_space=pltpu.VMEM)
     smem = pl.BlockSpec(memory_space=pltpu.SMEM)
+    anywhere = pl.BlockSpec(memory_space=pl.ANY)
     bf16, f32 = jnp.bfloat16, jnp.float32
-
-    def scratch(count, parts, rows, columns):
-        half = pltpu.VMEM((count, parts // 2, rows, columns), bf16)
-        return [pltpu.VMEM((count, parts, rows, columns), bf16), half, half, half]
-
-    def sems(count, kinds, parts):
-        return pltpu.SemaphoreType.DMA((count, kinds, parts // 2))
-
+    whole = (halves, n, chunk, width)
+    weights = (
+        triple_weight.transpose(0, 2, 1, 3),
+        output_weight,
+        upward_weight,
+        downward_weight,
+    )
+    results = [
+        jax.ShapeDtypeStruct(whole, bf16),
+        jax.ShapeDtypeStruct((LAYERS, 3, share, held_cols), f32),
+        jax.ShapeDtypeStruct((LAYERS, share, held_cols), f32),
+        jax.ShapeDtypeStruct((LAYERS, share, hidden), f32),
+        jax.ShapeDtypeStruct((LAYERS, share, hidden), f32),
+    ]
+
+    def grads(columns):
+        part = (LAYERS, m, share, columns)
+        half = pltpu.VMEM((LAYERS, m // 2, share, columns), bf16)
+        return [pltpu.VMEM(part, bf16), half, half, half, pltpu.SemaphoreType.DMA((LAYERS, 4, m // 2))]
+
+    half = pltpu.VMEM((sums, halves, n // 2, chunk, width), bf16)
+    full = pltpu.VMEM((sums,) + whole, bf16)
     outs = pl.pallas_call(
         functools.partial(kernel, n, m),
-        out_shape=[
-            jax.ShapeDtypeStruct((n, chunk, width), bf16),
-            jax.ShapeDtypeStruct((LAYERS, share, triple_cols), f32),
-            jax.ShapeDtypeStruct((LAYERS, share, held_cols), f32),
-            jax.ShapeDtypeStruct((LAYERS, share, hidden), f32),
-            jax.ShapeDtypeStruct((LAYERS, share, hidden), f32),
-        ],
-        in_specs=[smem] + [vmem] * 6,
-        out_specs=[vmem] * 5,
-        scratch_shapes=scratch(sums, n, chunk, width)
-        + [pltpu.VMEM((sums, n, chunk, width), bf16), sems(sums, 8, n)]
-        + scratch(LAYERS, m, share, 2 * hidden)
-        + [sems(LAYERS, 4, m)]
-        + scratch(LAYERS, m, share, held_cols)
-        + [sems(LAYERS, 4, m)]
-        + scratch(LAYERS, m, share, triple_cols)
-        + [sems(LAYERS, 4, m)]
+        out_shape=results,
+        in_specs=[smem, vmem, vmem] + [anywhere] * 4,
+        out_specs=[anywhere] * 5,
+        scratch_shapes=[pltpu.VMEM(weight.shape, bf16) for weight in weights]
+        + [pltpu.VMEM(result.shape, f32) for result in results[1:]]
+        + [
+            pltpu.SemaphoreType.DMA((LAYERS, 4)),
+            pltpu.SemaphoreType.DMA((LAYERS, 4)),
+            pltpu.SemaphoreType.DMA,
+        ]
+        + [full, half, half, half, full, pltpu.SemaphoreType.DMA((sums, halves, 8, n // 2))]
+        + grads(hidden)
+        + grads(hidden)
+        + grads(held_cols)
+        + grads(triple_cols)
         + [
             pltpu.VMEM((LAYERS, row_count, width), bf16),
             pltpu.VMEM((LAYERS, row_count, triple_cols), bf16),
@@ -489,24 +640,25 @@
             pltpu.VMEM((LAYERS, row_count, hidden), f32),
             pltpu.VMEM((LAYERS, row_count, hidden), bf16),
             pltpu.VMEM((row_count, hidden), bf16),
+            pltpu.VMEM((LAYERS, row_count, hidden), bf16),
+            pltpu.VMEM((row_count, held_cols), bf16),
             pltpu.VMEM((LAYERS, row_count, triple_cols), bf16),
         ],
         compiler_params=pltpu.CompilerParams(
-            collective_id=0, has_side_effects=True, vmem_limit_bytes=58 << 20
+            collective_id=0, has_side_effects=True, vmem_limit_bytes=60 << 20
         ),
-    )(
-        lengths,
-        tokens.reshape(n, chunk, width),
-        cotangent.reshape(n, chunk, width),
-        triple_weight.reshape(LAYERS, width, triple_cols),
-        output_weight,
-        upward_weight,
-        downward_weight,
-    )
-    final, triple, output, upward, downward = outs
+    )(lengths, tokens.reshape(whole), cotangent.reshape(whole), *weights)
+    most = max(result.shape[0] for result in results)
+    final, triple, output, upward, downward = pl.pallas_call(
+        hand_over,
+        out_shape=results,
+        in_specs=[anywhere] * 5,
+        out_specs=[anywhere] * 5,
+        scratch_shapes=[pltpu.SemaphoreType.DMA((5, most))],
+    )(*outs)
     return (
         final.reshape(row_count, width),
-        triple.reshape(LAYERS, share, 3, held_cols),
+        triple.transpose(0, 2, 1, 3),
         output,
         upward,
         downward,

time: 166 us -> 255 us (1.54)
  Pallas kernels: 155 us -> 254 us
  local copies, waits for them, and re-layouts: 9.36 us -> 0 us
    pallas_call x1 -> x2, Pallas kernels: 155 us -> 254 us  [the longest x1 141 us: body(): pl.pallas_call(functools.partial(kernel, n, m), out_shape=results, in_spe...]
    unnamed x14 -> x0, local copies, waits for them, and re-layouts: 6.31 us -> none
where the time goes in v3:
time: 255 us
  Pallas kernels  254 us (100%)
    pallas_call x1, Pallas kernels, body(): pl.pallas_call(functools.partial(kernel, n, m), out_shape=results, in_spe...  141 us
    pallas_call x1, Pallas kernels, body(): pl.pallas_call(hand_over, out_shape=results, in_specs=[anywhere] * 5, out...  112 us

profile of v3, /device:TPU:0, one launch (start us, length us, event | category | flops | bytes accessed | tf_op | source)
XLA Modules:
  0.0 255.0 jit_solution(6825896352313015480)
XLA Ops:
  1.3 141.1 %shard_map.110 = (bf16[2,8,16,1024]{3,2,1,0:T(8,128)(2,1)}, f32[2,3,256,128]{3,2,1,0:T(8,128)}, f32[2,256,128]{2,1,0:T(8,128)}, f32[2,256,512]{2,1,0:T(8,128)}, f32[2,256,512]{2,1,0:T(8,128)}) custom-call(s32[1]{0:T(128)S(6)} %copy.12.lengths, bf16[2,8,16,1024]{3,2,1,0:T(8,128)(2,1)} %bitcast.6, bf16[2,8,16,1024]{3,2,1,0:T(8,128)(2,1)} %bitcast.7, ...), custom_call_target="tpu_custom_call" | custom-call | tf_op jit(solution)/shard_map/pallas_call | solution.py:617
  142.4 112.4 %shard_map.111 = (bf16[2,8,16,1024]{3,2,1,0:T(8,128)(2,1)}, f32[2,3,256,128]{3,2,1,0:T(8,128)}, f32[2,256,128]{2,1,0:T(8,128)}, f32[2,256,512]{2,1,0:T(8,128)}, f32[2,256,512]{2,1,0:T(8,128)}) custom-call(bf16[2,8,16,1024]{3,2,1,0:T(8,128)(2,1)} %get-tuple-element.15.refs_0_, f32[2,3,256,128]{3,2,1,0:T(8,128)} %get-tuple-element.16.refs_1_, ...), custom_call_target="tpu_custom_call" | custom-call | tf_op jit(solution)/shard_map/pallas_call | solution.py:652

commit v4 on v3

--- a/solution.py
+++ b/solution.py
@@ -278,6 +278,7 @@
     held_cols = output_weight.shape[-1]
     heads = held_cols // HD
     me = lax.axis_index("mp")
+    query_rows = min(SLATE, half_rows)
     position = lax.broadcasted_iota(jnp.int32, (1, SLATE), 1)
 
     def rows(ref):
@@ -300,8 +301,19 @@
     def scatterer(refs, l):
         return Scatter("dp", m, *[ref.at[l] for ref in refs])
 
-    def put_grad(ref, l, value):
-        ref[l] = low(value).reshape(m, -1, value.shape[1])
+    def grad_work(ref, l, left, right, scatter):
+        share = width // m
+
+        def piece(d):
+            columns = slice(d * share, (d + 1) * share)
+            ref[l, d] = low(contract_rows(left(columns), right()))
+            if d == m - 1:
+                scatter.start()
+
+        return [functools.partial(piece, d) for d in range(m)]
+
+    def rows_of(ref):
+        return lambda columns: ref[:, :, :, columns].reshape(row_count, -1)
 
     def slices(s, h):
         block = slice(s * SLATE, (s + 1) * SLATE)
@@ -310,21 +322,27 @@
     def joined(l):
         return jnp.concatenate([triple_weight[l, i] for i in range(3)], axis=-1)
 
-    def nothing():
-        return None
-
     drained = []
     span = range(halves)
 
-    def close(k, steps, own, first_work=nothing, second_work=nothing):
+    def close(k, steps, own, work=()):
+        work = list(work)
+        points = 3 * halves
+        each = -(-len(work) // points)
+
+        def tick():
+            for _ in range(min(each, len(work))):
+                work.pop(0)()
+
         for step in steps:
+            tick()
             step.pass_on()
-        first_work()
         for a in span:
+            tick()
             whole[k, a, me] = low(own(a, steps[a].total()))
             steps[a].gather()
-        second_work()
         for step in steps:
+            tick()
             step.forward()
         drained.extend(steps)
 
@@ -349,19 +367,23 @@
                 arriving[a].finish()
             normed[l, cut(a)] = normalize(half(stream, a))[0]
             qkv[l, cut(a)] = low(dot(normed[l, cut(a)], joined(l)))
-        for s in range(slates):
-            live = wide(position < lengths[s])
-            for h in range(heads):
-                block, (q, k, v) = slices(s, h)
-                scores = contract_cols(qkv[l, block, q], qkv[l, block, k]) * HD ** (-0.5)
-                weights = jnp.exp(scores) * live
-                share = weights / jnp.sum(weights, axis=-1, keepdims=True)
-                probs[l, s * heads + h] = share
-                context[l, block, h * HD : (h + 1) * HD] = low(dot(low(share), qkv[l, block, v]))
         loads[l][1].wait()
         k_here = 2 * l
         steps = []
         for a in span:
+            for start in range(a * half_rows, (a + 1) * half_rows, query_rows):
+                s, offset = start // SLATE, start % SLATE
+                live = wide(position < lengths[s])
+                block = slice(start, start + query_rows)
+                for h in range(heads):
+                    keys, (q, k, v) = slices(s, h)
+                    scores = contract_cols(qkv[l, block, q], qkv[l, keys, k]) * HD ** (-0.5)
+                    weights = jnp.exp(scores) * live
+                    share = weights / jnp.sum(weights, axis=-1, keepdims=True)
+                    probs[l, s * heads + h, offset : offset + query_rows] = share
+                    context[l, block, h * HD : (h + 1) * HD] = low(
+                        dot(low(share), qkv[l, keys, v])
+                    )
             steps.append(opened(k_here, a, contract_cols(context[l, cut(a)], output_weight[l])))
             steps[a].start()
 
@@ -372,7 +394,7 @@
                 for a in span:
                     grad_act[cut(a)] = low(dot(half(cotangent, a), downward_weight[l]))
 
-        close(k_here, steps, added(stream), early)
+        close(k_here, steps, added(stream), [early])
         mid = whole.at[k_here]
         mids.append(mid)
         if l == LAYERS - 1:
@@ -478,25 +500,23 @@
         triple = scatterer((qkv_part, qkv_first, qkv_held, qkv_second, qkv_sems), l)
         drained += [down, up, att, triple]
 
-        def feed_grads(l=l, down=down, up=up, upstream=upstream):
-            put_grad(down_part, l, contract_rows(rows(upstream), activated[l]))
-            down.start()
-            put_grad(up_part, l, contract_rows(normed_mid[l], grad_preact[l]))
-            up.start()
-
-        def feed_pass(l=l, down=down, up=up):
-            down.pass_on()
-            up.pass_on()
-            if l == LAYERS - 1:
-                for a in span:
-                    opened(final_k, a, contract_cols(activated[l, cut(a)], downward_weight[l]))
-
-        close(k_next, steps, normed_back(mids[l], upstream), feed_grads, feed_pass)
+        def feed_final(a, l=l):
+            opened(final_k, a, contract_cols(activated[l, cut(a)], downward_weight[l]))
+
+        work = grad_work(down_part, l, rows_of(upstream), lambda l=l: activated[l], down)
+        work += grad_work(
+            up_part, l, lambda c, l=l: normed_mid[l, :, c], lambda l=l: grad_preact[l], up
+        )
+        work.append(down.pass_on)
+        if last:
+            work += [functools.partial(feed_final, a) for a in span]
+        close(k_next, steps, normed_back(mids[l], upstream), work)
         grad_mid = whole.at[k_next]
         k_next += 1
         for a in span:
             steps[a].finish()
             grad_context[cut(a)] = low(dot(half(grad_mid, a), output_weight[l]))
+        up.pass_on()
         advance()
         for s in range(slates):
             for h in range(heads):
@@ -510,30 +530,19 @@
                 grad_qkv[l, block, q] = low(dot(grad_score, qkv[l, block, k]))
                 grad_qkv[l, block, k] = low(contract_rows(grad_score, qkv[l, block, q]))
 
-        def att_grad(l=l, grad_mid=grad_mid, att=att):
-            put_grad(att_part, l, contract_rows(rows(grad_mid), context[l]))
-            att.start()
-
-        def triple_grad(l=l, triple=triple):
-            put_grad(qkv_part, l, contract_rows(normed[l], grad_qkv[l]))
-            triple.start()
-
+        att_work = grad_work(
+            att_part, l, rows_of(grad_mid), lambda l=l: context[l], att
+        )
+        triple_work = grad_work(
+            qkv_part, l, lambda c, l=l: normed[l, :, c], lambda l=l: grad_qkv[l], triple
+        )
         if l > 0:
             steps = []
             for a in span:
                 steps.append(opened(k_next, a, contract_cols(grad_qkv[l, cut(a)], joined(l))))
                 steps[a].start()
-
-            def attend_grads(att_grad=att_grad, triple_grad=triple_grad):
-                att_grad()
-                triple_grad()
-
-            def attend_pass(att=att, triple=triple):
-                att.pass_on()
-                triple.pass_on()
-                advance()
-
-            close(k_next, steps, normed_back(streams[l], grad_mid), attend_grads, attend_pass)
+            work = triple_work + att_work + [advance, triple.pass_on, att.pass_on]
+            close(k_next, steps, normed_back(streams[l], grad_mid), work)
             arriving = steps
             upstream = whole.at[k_next]
             k_next += 1
@@ -542,8 +551,8 @@
             pending.append(functools.partial(output_done, att, l))
             pending.append(functools.partial(triple_done, triple, l))
         else:
-            triple_grad()
-            att_grad()
+            for item in triple_work + att_work:
+                item()
             advance()
             triple.pass_on()
             att.pass_on()
@@ -563,16 +572,17 @@
 
 
 def hand_over(*refs):
-    count = (len(refs) - 1) // 2
-    sems = refs[-1]
-    copies = [
-        pltpu.make_async_copy(refs[i].at[j], refs[count + i].at[j], sems.at[i, j])
-        for i in range(count)
-        for j in range(refs[i].shape[0])
-    ]
-    for copy in copies:
+    count = (len(refs) - 1) // 3
+    sources, targets, staged, sems = refs[:count], refs[count : 2 * count], refs[2 * count : -1], refs[-1]
+    pairs = [(i, j) for i in range(count) for j in range(sources[i].shape[0])]
+    ins = [pltpu.make_async_copy(sources[i].at[j], staged[i].at[j], sems.at[0, i, j]) for i, j in pairs]
+    outs = [pltpu.make_async_copy(staged[i].at[j], targets[i].at[j], sems.at[1, i, j]) for i, j in pairs]
+    for copy in ins:
         copy.start()
-    for copy in copies:
+    for copy, onward in zip(ins, outs):
+        copy.wait()
+        onward.start()
+    for copy in outs:
         copy.wait()
 
 
@@ -654,7 +664,9 @@
         out_shape=results,
         in_specs=[anywhere] * 5,
         out_specs=[anywhere] * 5,
-        scratch_shapes=[pltpu.SemaphoreType.DMA((5, most))],
+        scratch_shapes=[pltpu.VMEM(result.shape, result.dtype) for result in results]
+        + [pltpu.SemaphoreType.DMA((2, 5, most))],
+        compiler_params=pltpu.CompilerParams(vmem_limit_bytes=16 << 20),
     )(*outs)
     return (
         final.reshape(row_count, width),

time: 255 us -> 149 us (0.58)
  Pallas kernels: 254 us -> 142 us
  local copies, waits for them, and re-layouts: 0 us -> 5.57 us
    pallas_call x1, Pallas kernels: 112 us -> 2.89 us  [body(): pl.pallas_call(hand_over, out_shape=results, in_specs=[anywhere] * 5, out...]
    unnamed x0 -> x10, local copies, waits for them, and re-layouts: none -> 5.57 us
where the time goes in v4:
time: 149 us
  Pallas kernels  142 us (95%)
  local copies, waits for them, and re-layouts  5.57 us (4%)
    pallas_call x1, Pallas kernels, body(): pl.pallas_call(functools.partial(kernel, n, m), out_shape=results, in_spe...  139 us
    unnamed x10, local copies, waits for them, and re-layouts  5.57 us

profile of v4, /device:TPU:0, one launch (start us, length us, event | category | flops | bytes accessed | tf_op | source)
XLA Modules:
  0.0 149.1 jit_solution(5544392111753245848)
XLA Ops:
  1.3 139.2 %shard_map.110 = (bf16[2,8,16,1024]{3,2,1,0:T(8,128)(2,1)}, f32[2,3,256,128]{3,2,1,0:T(8,128)}, f32[2,256,128]{2,1,0:T(8,128)}, f32[2,256,512]{2,1,0:T(8,128)}, f32[2,256,512]{2,1,0:T(8,128)}) custom-call(s32[1]{0:T(128)S(6)} %copy.12.lengths, bf16[2,8,16,1024]{3,2,1,0:T(8,128)(2,1)} %bitcast.6, bf16[2,8,16,1024]{3,2,1,0:T(8,128)(2,1)} %bitcast.7, ...), custom_call_target="tpu_custom_call" | custom-call | tf_op jit(solution)/shard_map/pallas_call | solution.py:627
  140.4 0.0 copy-start
  140.5 1.2 copy-done
  141.7 0.0 copy-start.1
  141.7 1.2 copy-done.1
  142.9 0.0 copy-start.2
  142.9 1.1 copy-done.2
  144.0 0.0 copy-start.3
  144.0 1.0 copy-done.3
  145.1 0.0 copy-start.4
  145.1 0.9 copy-done.4
  146.0 2.9 %shard_map.111 = (bf16[2,8,16,1024]{3,2,1,0:T(8,128)(2,1)}, f32[2,3,256,128]{3,2,1,0:T(8,128)}, f32[2,256,128]{2,1,0:T(8,128)}, f32[2,256,512]{2,1,0:T(8,128)}, f32[2,256,512]{2,1,0:T(8,128)}) custom-call(bf16[2,8,16,1024]{3,2,1,0:T(8,128)(2,1)S(1)} %copy-done.3, f32[2,3,256,128]{3,2,1,0:T(8,128)S(1)} %copy-done.2, f32[2,256,128]{2,1,0:T(8,128)S(1)} %copy-done.4, ...), custom_call_target="tpu_custom_call" | custom-call | tf_op jit(solution)/shard_map/pallas_call | solution.py:662
Async XLA Ops:
  140.4 1.2 copy-start
  141.7 1.2 copy-start.1
  142.9 1.1 copy-start.2
  144.0 1.0 copy-start.3
  145.1 0.9 copy-start.4

commit v5 on v4

--- a/solution.py
+++ b/solution.py
@@ -190,7 +190,7 @@
         for other in others:
             pl.semaphore_signal(barrier, inc=1, device_id={axis: other}, device_id_type=MESH)
         count += len(others)
-    pl.semaphore_wait(barrier, count)
+    return count
 
 
 def kernel(
@@ -270,7 +270,7 @@
     for layer_loads in loads:
         for copy in layer_loads:
             copy.start()
-    greet((("mp", n), ("dp", m)))
+    greeted = greet((("mp", n), ("dp", m)))
     halves, _, chunk, width = tokens.shape
     half_rows = n * chunk
     row_count = halves * half_rows
@@ -327,18 +327,17 @@
 
     def close(k, steps, own, work=()):
         work = list(work)
-        points = 3 * halves
-        each = -(-len(work) // points)
+        each = -(-len(work) // (2 * halves - 1))
 
         def tick():
             for _ in range(min(each, len(work))):
                 work.pop(0)()
 
         for step in steps:
-            tick()
             step.pass_on()
         for a in span:
-            tick()
+            if a > 0:
+                tick()
             whole[k, a, me] = low(own(a, steps[a].total()))
             steps[a].gather()
         for step in steps:
@@ -385,6 +384,8 @@
                         dot(low(share), qkv[l, keys, v])
                     )
             steps.append(opened(k_here, a, contract_cols(context[l, cut(a)], output_weight[l])))
+            if l == 0 and a == 0:
+                pl.semaphore_wait(pltpu.get_barrier_semaphore(), greeted)
             steps[a].start()
 
         def early(l=l):
@@ -666,7 +667,6 @@
         out_specs=[anywhere] * 5,
         scratch_shapes=[pltpu.VMEM(result.shape, result.dtype) for result in results]
         + [pltpu.SemaphoreType.DMA((2, 5, most))],
-        compiler_params=pltpu.CompilerParams(vmem_limit_bytes=16 << 20),
     )(*outs)
     return (
         final.reshape(row_count, width),

time: 149 us -> 147 us (0.987)
  local copies, waits for them, and re-layouts: 5.57 us -> 0 us
  Pallas kernels: 142 us -> 145 us
    unnamed x10 -> x0, local copies, waits for them, and re-layouts: 5.57 us -> none
    pallas_call x1, Pallas kernels: 139 us -> 142 us  [body(): pl.pallas_call(functools.partial(kernel, n, m), out_shape=results, in_spe...]
where the time goes in v5:
time: 147 us
  Pallas kernels  145 us (99%)
    pallas_call x1, Pallas kernels, body(): pl.pallas_call(functools.partial(kernel, n, m), out_shape=results, in_spe...  142 us
    pallas_call x1, Pallas kernels, body(): pl.pallas_call(hand_over, out_shape=results, in_specs=[anywhere] * 5, out...  3.29 us

profile of v5, /device:TPU:0, one launch (start us, length us, event | category | flops | bytes accessed | tf_op | source)
XLA Modules:
  0.0 146.6 jit_solution(7355807647584308366)
XLA Ops:
  1.3 141.8 %shard_map.110 = (bf16[2,8,16,1024]{3,2,1,0:T(8,128)(2,1)}, f32[2,3,256,128]{3,2,1,0:T(8,128)}, f32[2,256,128]{2,1,0:T(8,128)}, f32[2,256,512]{2,1,0:T(8,128)}, f32[2,256,512]{2,1,0:T(8,128)}) custom-call(s32[1]{0:T(128)S(6)} %copy.12.lengths, bf16[2,8,16,1024]{3,2,1,0:T(8,128)(2,1)} %bitcast.6, bf16[2,8,16,1024]{3,2,1,0:T(8,128)(2,1)} %bitcast.7, ...), custom_call_target="tpu_custom_call" | custom-call | tf_op jit(solution)/shard_map/pallas_call | solution.py:628
  143.1 3.3 %shard_map.111 = (bf16[2,8,16,1024]{3,2,1,0:T(8,128)(2,1)}, f32[2,3,256,128]{3,2,1,0:T(8,128)}, f32[2,256,128]{2,1,0:T(8,128)}, f32[2,256,512]{2,1,0:T(8,128)}, f32[2,256,512]{2,1,0:T(8,128)}) custom-call(bf16[2,8,16,1024]{3,2,1,0:T(8,128)(2,1)} %get-tuple-element.15.refs_0_, f32[2,3,256,128]{3,2,1,0:T(8,128)} %get-tuple-element.16.refs_1_, ...), custom_call_target="tpu_custom_call" | custom-call | tf_op jit(solution)/shard_map/pallas_call | solution.py:663

commit v6 on v5

--- a/solution.py
+++ b/solution.py
@@ -327,17 +327,17 @@
 
     def close(k, steps, own, work=()):
         work = list(work)
-        each = -(-len(work) // (2 * halves - 1))
+        each = -(-len(work) // (3 * halves))
 
         def tick():
             for _ in range(min(each, len(work))):
                 work.pop(0)()
 
         for step in steps:
+            tick()
             step.pass_on()
         for a in span:
-            if a > 0:
-                tick()
+            tick()
             whole[k, a, me] = low(own(a, steps[a].total()))
             steps[a].gather()
         for step in steps:

time: 147 us -> 145 us (0.986)
  Pallas kernels: 145 us -> 143 us
    pallas_call x1, Pallas kernels: 142 us -> 140 us  [body(): pl.pallas_call(functools.partial(kernel, n, m), out_shape=results, in_spe...]
where the time goes in v6:
time: 145 us
  Pallas kernels  143 us (99%)
  between operations  1.45 us (1%)
    pallas_call x1, Pallas kernels, body(): pl.pallas_call(functools.partial(kernel, n, m), out_shape=results, in_spe...  140 us
    pallas_call x1, Pallas kernels, body(): pl.pallas_call(hand_over, out_shape=results, in_specs=[anywhere] * 5, out...  3.29 us

profile of v6, /device:TPU:0, one launch (start us, length us, event | category | flops | bytes accessed | tf_op | source)
XLA Modules:
  0.0 144.9 jit_solution(7741839104323442955)
XLA Ops:
  1.3 140.1 %shard_map.110 = (bf16[2,8,16,1024]{3,2,1,0:T(8,128)(2,1)}, f32[2,3,256,128]{3,2,1,0:T(8,128)}, f32[2,256,128]{2,1,0:T(8,128)}, f32[2,256,512]{2,1,0:T(8,128)}, f32[2,256,512]{2,1,0:T(8,128)}) custom-call(s32[1]{0:T(128)S(6)} %copy.12.lengths, bf16[2,8,16,1024]{3,2,1,0:T(8,128)(2,1)} %bitcast.6, bf16[2,8,16,1024]{3,2,1,0:T(8,128)(2,1)} %bitcast.7, ...), custom_call_target="tpu_custom_call" | custom-call | tf_op jit(solution)/shard_map/pallas_call | solution.py:628
  141.4 3.3 %shard_map.111 = (bf16[2,8,16,1024]{3,2,1,0:T(8,128)(2,1)}, f32[2,3,256,128]{3,2,1,0:T(8,128)}, f32[2,256,128]{2,1,0:T(8,128)}, f32[2,256,512]{2,1,0:T(8,128)}, f32[2,256,512]{2,1,0:T(8,128)}) custom-call(bf16[2,8,16,1024]{3,2,1,0:T(8,128)(2,1)} %get-tuple-element.15.refs_0_, f32[2,3,256,128]{3,2,1,0:T(8,128)} %get-tuple-element.16.refs_1_, ...), custom_call_target="tpu_custom_call" | custom-call | tf_op jit(solution)/shard_map/pallas_call | solution.py:663
